TPU v7x, 1024 devices: a whole 8x8x8 slice. The times are simulated.
1024 devices in a mesh: face: 16 (over x, core), blk: 64 (over z, y).
Axes of the slice: x: 8, y: 8, z: 8, core: 2. Of those that a mesh axis runs over, the one named last changes fastest.
Arguments:
- tracer: float32 [512, 2048, 128], P('face', 'blk'), may hold values from -6 to 6
- wind_x: bfloat16 [512, 2048, 128], P('face', 'blk'), may hold values from -0.25 to 0.25
- wind_y: bfloat16 [512, 2048, 128], P('face', 'blk'), may hold values from -0.25 to 0.25
- cell_area: float32 [512, 2048], P('face', 'blk'), may hold values from 0.5 to 2
- forcing: bfloat16 [512, 2048, 384], P('face', 'blk'), may hold values from -6 to 6
- group_map: int32 [512, 2048], P('face', 'blk'), may hold values from -1 to 1023, as said below
- w_in: bfloat16 [64, 512, 512], P('blk'), may hold values from -0.375 to 0.375
- w_hidden: bfloat16 [64, 4, 512, 512], P('blk'), may hold values from -0.375 to 0.375
- w_out: bfloat16 [64, 512, 256], P('blk'), may hold values from -0.25 to 0.25
Outputs:
- advected: float32 [512, 2048, 128], P('face', 'blk')
- tendencies: bfloat16 [512, 2048, 256], P('face', 'blk')
Inputs may be any that keep to these rules, and one draw needn't show every extreme that they name: A column with group_map -1 is not called. Otherwise the value is d * 16 + p: the column goes to physics group d, held by blk index d with the same face index, at place p. The places that one device gives one group are 0 to n-1 without gaps, with n at most 16. Every group receives exactly 384 columns, from 25 devices of its blk group: all but two of them send exactly 16, the other two send amounts that add to 16.
All inputs are finite; a program needn't handle non-finite values.
Results may differ from a plain program's by a relative error of at most 0.0077.
Values may be sent and summed in bfloat16 or wider, within the bound.
No kernel may reach another device: no remote copies, remote signals or barrier semaphores. Data moves between devices by JAX's collectives and lax.ppermute only.
A program may use at most 32 MiB of HBM per device.

v0:
```python
import jax
import jax.numpy as jnp
from jax import lax
from jax.sharding import PartitionSpec as P


def extended(block, sides, width):
    for axis, dim in sides:
        count = lax.axis_size(axis)
        forward = [(i, i + 1) for i in range(count - 1)]
        forward.append((count - 1, 0))
        backward = [(target, source) for source, target in forward]
        low = lax.ppermute(
            lax.slice_in_dim(block, block.shape[dim] - width, None, axis=dim), axis, forward
        )
        high = lax.ppermute(lax.slice_in_dim(block, 0, width, axis=dim), axis, backward)
        block = jnp.concatenate([low, block, high], axis=dim)
    return block


def leaky_relu(values):
    return jnp.maximum(values, 0.15 * values)


def column_net(in_rows, w_in, w_hidden, w_out):
    hidden = leaky_relu(jnp.dot(in_rows, w_in, preferred_element_type=jnp.float32)).astype(
        jnp.bfloat16
    )
    for layer_index in range(w_hidden.shape[0]):
        hidden = leaky_relu(
            jnp.dot(hidden, w_hidden[layer_index], preferred_element_type=jnp.float32)
        ).astype(jnp.bfloat16)
    return jnp.dot(hidden, w_out, preferred_element_type=jnp.float32).astype(jnp.bfloat16)


def advect(tracer, wind_x, wind_y, cell_area):
    stacked = jnp.stack([tracer, wind_x.astype(jnp.float32), wind_y.astype(jnp.float32)])
    padded = extended(stacked, (("face", 1), ("blk", 2)), 1)
    middle = padded[0, 1:-1, 1:-1]
    speed_x = padded[1, 1:-1, 1:-1]
    speed_y = padded[2, 1:-1, 1:-1]
    east_flux = jnp.maximum(speed_x, 0.0) * middle + jnp.minimum(speed_x, 0.0) * padded[0, 2:, 1:-1]
    west_speed = padded[1, :-2, 1:-1]
    west_flux = (
        jnp.maximum(west_speed, 0.0) * padded[0, :-2, 1:-1] + jnp.minimum(west_speed, 0.0) * middle
    )
    north_flux = (
        jnp.maximum(speed_y, 0.0) * middle + jnp.minimum(speed_y, 0.0) * padded[0, 1:-1, 2:]
    )
    south_speed = padded[2, 1:-1, :-2]
    south_flux = (
        jnp.maximum(south_speed, 0.0) * padded[0, 1:-1, :-2]
        + jnp.minimum(south_speed, 0.0) * middle
    )
    spread = east_flux - west_flux + (north_flux - south_flux)
    return tracer - spread / cell_area[:, :, None]


def pack_slots(in_rows, send_slot, slot_total, groups):
    buffer = jnp.zeros((slot_total + 1, in_rows.shape[1]), in_rows.dtype).at[send_slot].set(in_rows)
    return buffer[:slot_total].reshape(groups, slot_total // groups, in_rows.shape[1])


def local(tracer, wind_x, wind_y, cell_area, forcing, group_map, w_in, w_hidden, w_out):
    groups = lax.axis_size("blk")
    cells_x, cells_y, levels = tracer.shape
    columns = cells_x * cells_y
    slots_per = columns // groups
    targets = group_map.reshape(columns)
    active = targets >= 0
    send_slot = jnp.where(active, targets, columns)
    forcing_rows = forcing.reshape(columns, forcing.shape[2])
    own_in = w_in[0]
    own_hidden = w_hidden[0]
    own_out = w_out[0]
    advected = advect(tracer, wind_x, wind_y, cell_area)
    features = jnp.concatenate(
        [advected.astype(jnp.bfloat16).reshape(columns, levels), forcing_rows], axis=1
    )
    received = lax.all_to_all(
        pack_slots(features, send_slot, columns, groups),
        "blk",
        split_axis=0,
        concat_axis=0,
        tiled=True,
    )
    feat_width = received.shape[2]
    result = column_net(received.reshape(-1, feat_width), own_in, own_hidden, own_out)
    slots_out = result.reshape(groups, slots_per, result.shape[1])
    returned = lax.all_to_all(slots_out, "blk", split_axis=0, concat_axis=0, tiled=True)
    returned_rows = returned.reshape(columns, returned.shape[2])
    returned_rows = jnp.concatenate(
        [returned_rows, jnp.zeros((1, returned_rows.shape[1]), jnp.bfloat16)], axis=0
    )
    tendencies = returned_rows[send_slot].reshape(cells_x, cells_y, returned_rows.shape[1])
    return (advected, tendencies)


def solution(mesh):
    placed = (
        P("face", "blk", None),
        P("face", "blk", None),
        P("face", "blk", None),
        P("face", "blk"),
        P("face", "blk", None),
        P("face", "blk"),
        P("blk", None, None),
        P("blk", None, None, None),
        P("blk", None, None),
    )
    return jax.shard_map(
        local,
        mesh=mesh,
        in_specs=placed,
        out_specs=(P("face", "blk", None), P("face", "blk", None)),
        check_vma=False,
    )
```

profile of v0, /device:TPU:14, one launch (start us, length us, event | category | flops | bytes accessed | tf_op | source)
XLA Modules:
  0.0 122.1 jit_solution(4404421797576513634)
XLA Ops:
  0.6 0.0 copy-start
  0.6 0.0 copy-start.1
  0.7 1.2 %convert_bitcast_fusion = (f32[1,32,32,128]{3,2,1,0:T(8,128)S(1)}, f32[1,32,32,128]{3,2,1,0:T(8,128)S(1)}) fusion(bf16[32,32,128]{2,1,0:T(8,128)(2,1)} %param.11, bf16[32,32,128]{2,1,0:T(8,128)(2,1)} %param.10), kind=kLoop, calls=%fused_computation.26 | loop fusion | flops 262144 | bytes 1572864 | tf_op jit(solution)/shard_map/stack | solution.py:37
  1.9 0.0 copy-start.2
  1.9 0.0 copy-start.3
  2.0 0.8 pad_maximum_fusion.23
  2.8 1.7 %collective-permute-start = (f32[3,1,32,128]{3,2,1,0:T(8,128)S(1)}, f32[3,1,32,128]{3,2,1,0:T(8,128)S(1)}, u32[]{:S(2)}, u32[]{:S(2)}) collective-permute-start(f32[3,1,32,128]{3,2,1,0:T(8,128)S(1)} %get-tuple-element.7), channel_id=1, source_target_pairs={{64,0},{128,64},{192,128},{256,192},{320,256},{384,320},{448,384},... | collective-permute-start | bytes 147464 | tf_op jit(solution)/shard_map/ppermute | solution.py:16
  4.5 0.1 reshape.75
  4.6 1.7 %collective-permute-done.1 = f32[3,1,32,128]{3,2,1,0:T(8,128)S(1)} collective-permute-done((f32[3,1,32,128]{3,2,1,0:T(8,128)S(1)}, f32[3,1,32,128]{3,2,1,0:T(8,128)S(1)}, u32[]{:S(2)}, u32[]{:S(2)}) %collective-permute-start.1) | collective-permute-done | bytes 49184 | tf_op jit(solution)/shard_map/ppermute | solution.py:13
  6.3 10.3 %collective-permute-done = f32[3,1,32,128]{3,2,1,0:T(8,128)S(1)} collective-permute-done((f32[3,1,32,128]{3,2,1,0:T(8,128)S(1)}, f32[3,1,32,128]{3,2,1,0:T(8,128)S(1)}, u32[]{:S(2)}, u32[]{:S(2)}) %collective-permute-start) | collective-permute-done | bytes 49184 | tf_op jit(solution)/shard_map/ppermute | solution.py:16
  16.6 0.1 pad_maximum_fusion.22
  16.7 10.7 %collective-permute-start.2 = (f32[3,34,1,128]{3,2,1,0:T(1,128)S(1)}, f32[3,34,1,128]{3,2,1,0:T(1,128)S(1)}, u32[]{:S(2)}, u32[]{:S(2)}) collective-permute-start(f32[3,34,1,128]{3,2,1,0:T(1,128)S(1)} %get-tuple-element.4), channel_id=1, source_target_pairs={{1,0},{2,1},{3,2},{4,3},{5,4},{6,5},{7,6},{8,7},{9,8},{10,9},{11,1... | collective-permute-start | bytes 156680 | tf_op jit(solution)/shard_map/ppermute | solution.py:16
  27.4 1.9 %collective-permute-start.3 = (f32[3,34,1,128]{3,2,1,0:T(1,128)S(1)}, f32[3,34,1,128]{3,2,1,0:T(1,128)S(1)}, u32[]{:S(2)}, u32[]{:S(2)}) collective-permute-start(f32[3,34,1,128]{3,2,1,0:T(1,128)S(1)} %get-tuple-element.5), channel_id=1, source_target_pairs={{0,1},{1,2},{2,3},{3,4},{4,5},{5,6},{6,7},{7,8},{8,9},{9,10},{10,1... | collective-permute-start | bytes 156680 | tf_op jit(solution)/shard_map/ppermute | solution.py:13
  29.3 7.6 %collective-permute-done.3 = f32[3,34,1,128]{3,2,1,0:T(1,128)S(1)} collective-permute-done((f32[3,34,1,128]{3,2,1,0:T(1,128)S(1)}, f32[3,34,1,128]{3,2,1,0:T(1,128)S(1)}, u32[]{:S(2)}, u32[]{:S(2)}) %collective-permute-start.3) | collective-permute-done | bytes 52256 | tf_op jit(solution)/shard_map/ppermute | solution.py:13
  36.9 2.2 %fusion.75 = (bf16[32,32,128]{2,1,0:T(8,128)(2,1)S(1)}, f32[32,32,128]{2,1,0:T(8,128)}) fusion(f32[32,32,128]{2,1,0:T(8,128)S(1)} %copy-done.1, f32[32,32]{1,0:T(8,128)S(1)} %copy-done.4, f32[3,1,32,128]{3,2,1,0:T(8,128)S(1)} %collective-permute-done, f32[1,32,32,128]{3,2,1,0:T(8,128)S(1)} %get-tuple-element.8, f32[1,32,32,128]{3,2,1,0:T(8,128)S(1)} %get-tuple-element.9, ...), kind=kLoop, calls=%fused_computation.95 | loop fusion | flops 6815744 | bytes 3614720 | tf_op jit(solution)/shard_map/convert_element_type | solution.py:78
  39.1 5.8 %scatter_custom_fusion = bf16[1025,512]{1,0:T(8,128)(2,1)S(1)} fusion(s32[1024]{0:T(1024)S(1)} %bitcast.82, bf16[1024,384]{1,0:T(8,128)(2,1)} %bitcast.80, bf16[]{:T(256)} %constant.24, bf16[1024,128]{1,0:T(8,128)(2,1)S(1)} %bitcast.79, bf16[]{:T(256)} %constant.0.clone.1), kind=kCustom, calls=%fused_computation.17 | custom fusion | flops 2097152 | bytes 2098180 | tf_op jit(solution)/shard_map/scatter | solution.py:60
  44.9 0.1 slice.72
  44.9 34.1 %all_to_all.10 = bf16[64,16,512]{2,1,0:T(8,128)(2,1)S(1)} all-to-all(bf16[64,16,512]{2,1,0:T(8,128)(2,1)S(1)} %bitcast.76), channel_id=1, replica_groups=mesh['face'=16,'blk'=64] {'blk'}, dimensions={0} | all-to-all | bytes 2097152 | tf_op jit(solution)/shard_map/all_to_all | solution.py:80
  79.1 3.6 %fusion.20 = f32[1024,512]{1,0:T(8,128)} fusion(bf16[1024,512]{1,0:T(8,128)(2,1)S(1)} %bitcast.78, bf16[1,512,512]{2,1,0:T(8,128)(2,1)S(1)} %copy-done, bf16[1,4,512,512]{3,2,1,0:T(8,128)(2,1)} %param.16), kind=kOutput, calls=%fused_computation.16 | convolution fusion | flops 1075314688 | bytes 4194304 | tf_op jit(solution)/shard_map/dot_general | solution.py:31
  82.7 4.4 %fusion.12 = f32[1024,512]{1,0:T(8,128)} fusion(f32[1024,512]{1,0:T(8,128)} %fusion.20, bf16[1,4,512,512]{3,2,1,0:T(8,128)(2,1)} %param.16), kind=kOutput, calls=%fused_computation.14 | convolution fusion | flops 1076887552 | bytes 5242880 | tf_op jit(solution)/shard_map/dot_general | solution.py:31
  87.1 3.6 %convolution_convert_fusion = bf16[1024,256]{1,0:T(8,128)(2,1)} fusion(f32[1024,512]{1,0:T(8,128)} %fusion.12, bf16[1,4,512,512]{3,2,1,0:T(8,128)(2,1)} %param.16, bf16[1,512,256]{2,1,0:T(8,128)(2,1)S(1)} %copy-done.6), kind=kOutput, calls=%fused_computation.12 | convolution fusion | flops 808714240 | bytes 3407872 | tf_op jit(solution)/shard_map/dot_general | solution.py:33
  90.7 7.1 %all-to-all-start.1 = ((bf16[64,16,256]{2,1,0:T(8,128)(2,1)}), bf16[64,16,256]{2,1,0:T(8,128)(2,1)S(1)}, u32[]{:S(2)}, u32[]{:S(2)}) async-start(bf16[64,16,256]{2,1,0:T(8,128)(2,1)} %bitcast.20), calls=%async_computation.1 | async-start | bytes 1048576 | tf_op jit(solution)/shard_map/all_to_all | solution.py:90
  97.9 19.2 %all-to-all-done.1 = bf16[64,16,256]{2,1,0:T(8,128)(2,1)S(1)} async-done(((bf16[64,16,256]{2,1,0:T(8,128)(2,1)}), bf16[64,16,256]{2,1,0:T(8,128)(2,1)S(1)}, u32[]{:S(2)}, u32[]{:S(2)}) %all-to-all-start.1) | async-done | bytes 524320 | tf_op jit(solution)/shard_map/all_to_all | solution.py:90
  117.1 5.0 %gather_fusion = bf16[1024,256]{1,0:T(8,128)(2,1)} fusion(bf16[1025,256]{1,0:T(8,128)(2,1)S(1)} %concatenate.30, s32[1024]{0:T(1024)S(1)} %broadcast_clamp_fusion), kind=kCustom, calls=%fused_computation | custom fusion | bytes 1052672 | tf_op jit(solution)/shard_map/gather | solution.py:95
  (15 shorter events, 0.1 us)
Async XLA Ops:
  0.6 78.4 %copy-start = (bf16[1,512,512]{2,1,0:T(8,128)(2,1)S(1)}, bf16[1,512,512]{2,1,0:T(8,128)(2,1)}, u32[]{:S(2)}) copy-start(bf16[1,512,512]{2,1,0:T(8,128)(2,1)} %param.15) | copy-start | bytes 1572868
  0.6 16.0 %copy-start.1 = (f32[32,32,128]{2,1,0:T(8,128)S(1)}, f32[32,32,128]{2,1,0:T(8,128)}, u32[]{:S(2)}) copy-start(f32[32,32,128]{2,1,0:T(8,128)} %param.9) | copy-start | bytes 1572868
  0.7 3.8 %copy-start.5 = (s32[32,32]{1,0:T(8,128)S(1)}, s32[32,32]{1,0:T(8,128)}, u32[]{:S(2)}) copy-start(s32[32,32]{1,0:T(8,128)} %param.14) | copy-start | bytes 12292
  1.9 35.0 %copy-start.2 = (bf16[32,32,128]{2,1,0:T(8,128)(2,1)S(1)}, bf16[32,32,128]{2,1,0:T(8,128)(2,1)}, u32[]{:S(2)}) copy-start(bf16[32,32,128]{2,1,0:T(8,128)(2,1)} %param.11) | copy-start | bytes 786436
  1.9 35.0 %copy-start.3 = (bf16[32,32,128]{2,1,0:T(8,128)(2,1)S(1)}, bf16[32,32,128]{2,1,0:T(8,128)(2,1)}, u32[]{:S(2)}) copy-start(bf16[32,32,128]{2,1,0:T(8,128)(2,1)} %param.10) | copy-start | bytes 786436
  1.9 35.0 %copy-start.4 = (f32[32,32]{1,0:T(8,128)S(1)}, f32[32,32]{1,0:T(8,128)}, u32[]{:S(2)}) copy-start(f32[32,32]{1,0:T(8,128)} %param.12) | copy-start | bytes 12292
  2.7 3.5 %collective-permute-start.1 = (f32[3,1,32,128]{3,2,1,0:T(8,128)S(1)}, f32[3,1,32,128]{3,2,1,0:T(8,128)S(1)}, u32[]{:S(2)}, u32[]{:S(2)}) collective-permute-start(f32[3,1,32,128]{3,2,1,0:T(8,128)S(1)} %get-tuple-element.6), channel_id=1, source_target_pairs={{0,64},{64,128},{128,192},{192,256},{256,320},{320,384},{384,448},... | collective-permute-start | bytes 147464 | tf_op jit(solution)/shard_map/ppermute | solution.py:13
  2.8 13.8 %collective-permute-start = (f32[3,1,32,128]{3,2,1,0:T(8,128)S(1)}, f32[3,1,32,128]{3,2,1,0:T(8,128)S(1)}, u32[]{:S(2)}, u32[]{:S(2)}) collective-permute-start(f32[3,1,32,128]{3,2,1,0:T(8,128)S(1)} %get-tuple-element.7), channel_id=1, source_target_pairs={{64,0},{128,64},{192,128},{256,192},{320,256},{384,320},{448,384},... | collective-permute-start | bytes 147464 | tf_op jit(solution)/shard_map/ppermute | solution.py:16
  16.7 12.6 %collective-permute-start.2 = (f32[3,34,1,128]{3,2,1,0:T(1,128)S(1)}, f32[3,34,1,128]{3,2,1,0:T(1,128)S(1)}, u32[]{:S(2)}, u32[]{:S(2)}) collective-permute-start(f32[3,34,1,128]{3,2,1,0:T(1,128)S(1)} %get-tuple-element.4), channel_id=1, source_target_pairs={{1,0},{2,1},{3,2},{4,3},{5,4},{6,5},{7,6},{8,7},{9,8},{10,9},{11,1... | collective-permute-start | bytes 156680 | tf_op jit(solution)/shard_map/ppermute | solution.py:16
  27.4 9.5 %collective-permute-start.3 = (f32[3,34,1,128]{3,2,1,0:T(1,128)S(1)}, f32[3,34,1,128]{3,2,1,0:T(1,128)S(1)}, u32[]{:S(2)}, u32[]{:S(2)}) collective-permute-start(f32[3,34,1,128]{3,2,1,0:T(1,128)S(1)} %get-tuple-element.5), channel_id=1, source_target_pairs={{0,1},{1,2},{2,3},{3,4},{4,5},{5,6},{6,7},{7,8},{8,9},{9,10},{10,1... | collective-permute-start | bytes 156680 | tf_op jit(solution)/shard_map/ppermute | solution.py:13
  82.7 4.5 %copy-start.6 = (bf16[1,512,256]{2,1,0:T(8,128)(2,1)S(1)}, bf16[1,512,256]{2,1,0:T(8,128)(2,1)}, u32[]{:S(2)}) copy-start(bf16[1,512,256]{2,1,0:T(8,128)(2,1)} %param.17) | copy-start | bytes 786436
  90.7 26.3 %all-to-all-start.1 = ((bf16[64,16,256]{2,1,0:T(8,128)(2,1)}), bf16[64,16,256]{2,1,0:T(8,128)(2,1)S(1)}, u32[]{:S(2)}, u32[]{:S(2)}) async-start(bf16[64,16,256]{2,1,0:T(8,128)(2,1)} %bitcast.20), calls=%async_computation.1 | async-start | bytes 1048576 | tf_op jit(solution)/shard_map/all_to_all | solution.py:90
where the time goes:
time: 123 us; the launch traced here: 122 us
  waiting for transfers between devices  38.8 us (32%)
  blocking collectives  34.1 us (28%)
  starting transfers between devices  21.5 us (17%)
  matrix products  11.7 us (10%)
  other arithmetic  10.1 us (8%)
  local copies, waits for them, and re-layouts  5.21 us (4%)
    all_to_all x1, blocking collectives, local(): lax.all_to_all(pack_slots(features, send_slot, columns, groups), 'blk', s...  34.1 us
    all_to_all x1, waiting for transfers between devices, local(): lax.all_to_all(slots_out, 'blk', split_axis=0, concat_axis=0, tiled=True)  19.2 us
    ppermute x2, starting transfers between devices, extended(): lax.ppermute(lax.slice_in_dim(block, 0, width, axis=dim), axis, backward)  12.4 us
    ppermute x2, waiting for transfers between devices, extended(): lax.ppermute(lax.slice_in_dim(block, 0, width, axis=dim), axis, backward)  10.3 us
    ppermute x2, waiting for transfers between devices, extended(): lax.ppermute(lax.slice_in_dim(block, block.shape[dim] - width, None, axis...  9.27 us
    dot_general x2, matrix products, column_net(): jnp.dot(hidden, w_hidden[layer_index], preferred_element_type=jnp.float32)  8.07 us
    all_to_all x1, starting transfers between devices, local(): lax.all_to_all(slots_out, 'blk', split_axis=0, concat_axis=0, tiled=True)  7.15 us
    scatter x1, other arithmetic, pack_slots(): jnp.zeros((slot_total + 1, in_rows.shape[1]), in_rows.dtype).at[send_slot]  5.77 us
  transfers between devices with their start and end apart: 5, of which 4 were waited for; matrix products, arithmetic and copies ran while one was open for 0% of the time, Pallas kernels for 0%

commit v1 on v0

v1 whole, which is shorter than its diff:
```python
import jax
import jax.numpy as jnp
from jax import lax
from jax.experimental import pallas as pl
from jax.experimental.pallas import tpu as pltpu
from jax.sharding import PartitionSpec as P

SLOPE = 0.15
VMEM = pl.BlockSpec(memory_space=pltpu.VMEM)


def call(kernel, outs, operands, name, flops=0, touched=0, scratch=(), limit=48 << 20):
    return pl.pallas_call(
        kernel,
        out_shape=outs,
        in_specs=[VMEM] * len(operands),
        out_specs=jax.tree.map(lambda _: VMEM, outs),
        scratch_shapes=list(scratch),
        compiler_params=pltpu.CompilerParams(vmem_limit_bytes=limit),
        cost_estimate=pl.CostEstimate(flops=flops, bytes_accessed=touched, transcendentals=0),
        name=name,
    )(*operands)


def edges_kernel(tracer, wind_x, wind_y, last_x, first_x, last_y, first_y):
    cells_x, cells_y, _ = tracer.shape
    last_x[0] = tracer[cells_x - 1]
    last_x[1] = wind_x[cells_x - 1].astype(jnp.float32)
    first_x[...] = tracer[0]
    last_y[0] = tracer[:, cells_y - 1, :]
    last_y[1] = wind_y[...].astype(jnp.float32)[:, cells_y - 1, :]
    first_y[...] = tracer[:, 0, :]


def select_kernel(target_row, target_column, forcing, to_slots, to_columns, packed):
    slots, columns = to_slots.shape
    step = 256

    def body(index, _):
        rows = pl.ds(pl.multiple_of(index * step, step), step)
        place = lax.broadcasted_iota(jnp.int32, (step, columns), 0) + index * step
        picked = jnp.where(target_row[...] == place, 1.0, 0.0).astype(jnp.bfloat16)
        to_slots[rows, :] = picked
        packed[rows, :] = jnp.dot(
            picked, forcing[...], preferred_element_type=jnp.float32
        ).astype(jnp.bfloat16)
        place = lax.broadcasted_iota(jnp.int32, (step, slots), 1)
        to_columns[rows, :] = jnp.where(target_column[rows, :] == place, 1.0, 0.0).astype(
            jnp.bfloat16
        )
        return 0

    lax.fori_loop(0, slots // step, body, 0)


def advect_kernel(
    tracer,
    wind_x,
    wind_y,
    area_t,
    west,
    east,
    south,
    north,
    to_slots,
    packed_forcing,
    advected,
    features,
    rounded,
):
    cells_x, cells_y, levels = tracer.shape
    inverse = 1.0 / area_t[...]
    place = lax.broadcasted_iota(jnp.int32, (cells_y, levels), 0)
    west_speed = west[1]
    flux_before = jnp.maximum(west_speed, 0.0) * west[0] + jnp.minimum(west_speed, 0.0) * tracer[0]
    for i in range(cells_x):
        here = tracer[i]
        after = tracer[i + 1] if i + 1 < cells_x else east[...]
        speed = wind_x[i].astype(jnp.float32)
        flux_x = jnp.maximum(speed, 0.0) * here + jnp.minimum(speed, 0.0) * after
        speed = wind_y[i].astype(jnp.float32)
        beyond = jnp.where(
            place == cells_y - 1, north[i : i + 1, :], pltpu.roll(here, cells_y - 1, 0)
        )
        flux_y = jnp.maximum(speed, 0.0) * here + jnp.minimum(speed, 0.0) * beyond
        south_speed = south[1, i : i + 1, :]
        south_flux = (
            jnp.maximum(south_speed, 0.0) * south[0, i : i + 1, :]
            + jnp.minimum(south_speed, 0.0) * here[0:1, :]
        )
        flux_y_before = jnp.where(place == 0, south_flux, pltpu.roll(flux_y, 1, 0))
        spread = (flux_x - flux_before) + (flux_y - flux_y_before)
        moved = here - spread * inverse[:, i : i + 1]
        advected[i] = moved
        rounded[i * cells_y : (i + 1) * cells_y, :] = moved.astype(jnp.bfloat16)
        flux_before = flux_x
    features[:, levels:] = packed_forcing[...]
    features[:, :levels] = jnp.dot(
        to_slots[...], rounded[...], preferred_element_type=jnp.float32
    ).astype(jnp.bfloat16)


def net_kernel(rows_in, w_in, w_hidden, w_out, result):
    step = 256

    def leaky(values):
        return jnp.maximum(values, SLOPE * values).astype(jnp.bfloat16)

    def body(index, _):
        rows = pl.ds(pl.multiple_of(index * step, step), step)
        hidden = leaky(jnp.dot(rows_in[rows, :], w_in[0], preferred_element_type=jnp.float32))
        for layer in range(w_hidden.shape[1]):
            hidden = leaky(
                jnp.dot(hidden, w_hidden[0, layer], preferred_element_type=jnp.float32)
            )
        result[rows, :] = jnp.dot(
            hidden, w_out[0], preferred_element_type=jnp.float32
        ).astype(jnp.bfloat16)
        return 0

    lax.fori_loop(0, rows_in.shape[0] // step, body, 0)


def unpack_kernel(to_columns, returned, tendencies):
    step = 256

    def body(index, _):
        rows = pl.ds(pl.multiple_of(index * step, step), step)
        tendencies[rows, :] = jnp.dot(
            to_columns[rows, :], returned[...], preferred_element_type=jnp.float32
        ).astype(jnp.bfloat16)
        return 0

    lax.fori_loop(0, tendencies.shape[0] // step, body, 0)


def neighbours(axis):
    count = lax.axis_size(axis)
    forward = [(i, (i + 1) % count) for i in range(count)]
    return forward, [(target, source) for source, target in forward]


def local(tracer, wind_x, wind_y, cell_area, forcing, group_map, w_in, w_hidden, w_out):
    groups = lax.axis_size("blk")
    cells_x, cells_y, levels = tracer.shape
    columns = cells_x * cells_y
    slots_per = columns // groups
    width = levels + forcing.shape[2]
    width_out = w_out.shape[2]
    f32, bf16 = jnp.float32, jnp.bfloat16
    shaped = jax.ShapeDtypeStruct

    last_x, first_x, last_y, first_y = call(
        edges_kernel,
        [
            shaped((2, cells_y, levels), f32),
            shaped((cells_y, levels), f32),
            shaped((2, cells_x, levels), f32),
            shaped((cells_x, levels), f32),
        ],
        [tracer, wind_x, wind_y],
        "edges",
        touched=1 << 20,
    )
    forward, backward = neighbours("face")
    west = lax.ppermute(last_x, "face", forward)
    east = lax.ppermute(first_x, "face", backward)
    forward, backward = neighbours("blk")
    south = lax.ppermute(last_y, "blk", forward)
    north = lax.ppermute(first_y, "blk", backward)

    to_slots, to_columns, packed_forcing = call(
        select_kernel,
        [
            shaped((columns, columns), bf16),
            shaped((columns, columns), bf16),
            shaped((columns, forcing.shape[2]), bf16),
        ],
        [
            group_map.reshape(1, columns),
            group_map.reshape(columns, 1),
            forcing.reshape(columns, forcing.shape[2]),
        ],
        "select",
        flops=2 * columns * columns * forcing.shape[2],
        touched=6 << 20,
    )
    advected, features = call(
        advect_kernel,
        [shaped(tracer.shape, f32), shaped((columns, width), bf16)],
        [
            tracer,
            wind_x,
            wind_y,
            cell_area.T,
            west,
            east,
            south,
            north,
            to_slots,
            packed_forcing,
        ],
        "advect",
        flops=2 * columns * columns * levels,
        touched=6 << 20,
        scratch=[pltpu.VMEM((columns, levels), bf16)],
    )
    received = lax.all_to_all(
        features.reshape(groups, slots_per, width), "blk", split_axis=0, concat_axis=0, tiled=True
    )
    result = call(
        net_kernel,
        shaped((columns, width_out), bf16),
        [received.reshape(columns, width), w_in, w_hidden, w_out],
        "net",
        flops=2 * columns * (w_in.size + w_hidden.size + w_out.size),
        touched=5 << 20,
    )
    returned = lax.all_to_all(
        result.reshape(groups, slots_per, width_out), "blk", split_axis=0, concat_axis=0, tiled=True
    )
    tendencies = call(
        unpack_kernel,
        shaped((columns, width_out), bf16),
        [to_columns, returned.reshape(columns, width_out)],
        "unpack",
        flops=2 * columns * columns * width_out,
        touched=3 << 20,
    )
    return advected, tendencies.reshape(cells_x, cells_y, width_out)


def solution(mesh):
    placed = (
        P("face", "blk", None),
        P("face", "blk", None),
        P("face", "blk", None),
        P("face", "blk"),
        P("face", "blk", None),
        P("face", "blk"),
        P("blk", None, None),
        P("blk", None, None, None),
        P("blk", None, None),
    )
    return jax.shard_map(
        local,
        mesh=mesh,
        in_specs=placed,
        out_specs=(P("face", "blk", None), P("face", "blk", None)),
        check_vma=False,
    )
```

time: 123 us -> 113 us (0.919)
  waiting for transfers between devices: 38.8 us -> 0.01 us
  blocking collectives: 34.1 us -> 65.4 us
  Pallas kernels: 0 us -> 11.8 us
  matrix products: 11.7 us -> 0 us
  other arithmetic: 10.1 us -> 0 us
  local copies, waits for them, and re-layouts: 5.21 us -> 10.1 us
  starting transfers between devices: 21.5 us -> 23.8 us
    all_to_all x1 -> x2, blocking collectives: 34.1 us -> 65.4 us  [the longest x1 37.7 us: local(): lax.all_to_all(features.reshape(groups, slots_per, width), 'blk', split_a...]
    ppermute x4, waiting for transfers between devices: 19.6 us -> 0.01 us  [the longest x1 0.01 us: local(): east = lax.ppermute(first_x, 'face', backward)]
    all_to_all x1 -> x0, waiting for transfers between devices: 19.2 us -> none  [local(): lax.all_to_all(slots_out, 'blk', split_axis=0, concat_axis=0, tiled=True)]
    pallas_call x0 -> x5, Pallas kernels: none -> 11.8 us  [call(): pl.pallas_call(kernel, out_shape=outs, in_specs=[VMEM] * len(operands), o...]
    dot_general x3 -> x0, matrix products: 11.7 us -> none  [the longest x2 8.07 us: column_net(): jnp.dot(hidden, w_hidden[layer_index], preferred_element_type=jnp.float32)]
    ppermute x4, starting transfers between devices: 14.3 us -> 23.8 us  [the longest x1 21 us: local(): north = lax.ppermute(first_y, 'blk', backward)]
    unnamed x14 -> x31, local copies, waits for them, and re-layouts: 0.04 us -> 7.22 us
    all_to_all x1 -> x0, starting transfers between devices: 7.15 us -> none  [local(): lax.all_to_all(slots_out, 'blk', split_axis=0, concat_axis=0, tiled=True)]
  transfers between devices with their start and end apart: 5 -> 4, of which waited for: 4 -> 0; matrix products, arithmetic and copies ran while one was open for 0% -> 3% of each run, Pallas kernels for 0% -> 3%
where the time goes in v1:
time: 113 us; the launch traced here: 112 us
  blocking collectives  65.4 us (58%)
  starting transfers between devices  23.8 us (21%)
  Pallas kernels  11.8 us (10%)
  local copies, waits for them, and re-layouts  10.1 us (9%)
    all_to_all x1, blocking collectives, local(): lax.all_to_all(features.reshape(groups, slots_per, width), 'blk', split_a...  37.7 us
    all_to_all x1, blocking collectives, local(): lax.all_to_all(result.reshape(groups, slots_per, width_out), 'blk', split...  27.7 us
    ppermute x1, starting transfers between devices, local(): north = lax.ppermute(first_y, 'blk', backward)  21 us
    pallas_call x5, Pallas kernels, call(): pl.pallas_call(kernel, out_shape=outs, in_specs=[VMEM] * len(operands), o...  11.8 us
    unnamed x31, local copies, waits for them, and re-layouts  7.22 us
  transfers between devices with their start and end apart: 4, of which 0 were waited for; matrix products, arithmetic and copies ran while one was open for 3% of the time, Pallas kernels for 3%

profile of v1, /device:TPU:14, one launch (start us, length us, event | category | flops | bytes accessed | tf_op | source)
XLA Modules:
  0.0 111.9 jit_solution(14873062318966980635)
XLA Ops:
  0.6 1.0 copy-done.1
  1.7 0.9 copy-done.3
  2.6 0.9 copy-done.5
  3.6 0.9 collective-permute-start.1
  4.5 21.0 %collective-permute-start.3 = (f32[32,128]{1,0:T(8,128)S(1)}, f32[32,128]{1,0:T(8,128)S(1)}, u32[]{:S(2)}, u32[]{:S(2)}) collective-permute-start(f32[32,128]{1,0:T(8,128)S(1)} %get-tuple-element.14), channel_id=1, source_target_pairs={{1,0},{2,1},{3,2},{4,3},{5,4},{6,5},{7,6},{8,7},{9,8},{10,9},{11,1... | collective-permute-start | bytes 49160 | tf_op jit(solution)/shard_map/ppermute | solution.py:170
  25.5 0.0 collective-permute-start
  25.6 1.9 %collective-permute-start.2 = (f32[2,32,128]{2,1,0:T(8,128)S(1)}, f32[2,32,128]{2,1,0:T(8,128)S(1)}, u32[]{:S(2)}, u32[]{:S(2)}) collective-permute-start(f32[2,32,128]{2,1,0:T(8,128)S(1)} %get-tuple-element.13), channel_id=1, source_target_pairs={{0,1},{1,2},{2,3},{3,4},{4,5},{5,6},{6,7},{7,8},{8,9},{9,10},{10,1... | collective-permute-start | bytes 98312 | tf_op jit(solution)/shard_map/ppermute | solution.py:169
  27.5 0.8 reshape.28.target_row
  28.3 2.0 %reshape.36.target_column = s32[1024,1]{1,0:T(8,128)} reshape(s32[32,32]{1,0:T(8,128)} %param.14) | data formatting | bytes 8192 | tf_op jit(solution)/shard_map/reshape | solution.py:181
  30.3 1.0 copy-done.9
  31.4 1.1 %copy-done.11 = bf16[32,32,384]{2,1,0:T(8,128)(2,1)S(1)} copy-done((bf16[32,32,384]{2,1,0:T(8,128)(2,1)S(1)}, bf16[32,32,384]{2,1,0:T(8,128)(2,1)}, u32[]{:S(2)}) %copy-start.11) | copy-done | bytes 786456
  32.5 3.1 %select.1 = (bf16[1024,1024]{1,0:T(8,128)(2,1)S(1)}, bf16[1024,1024]{1,0:T(8,128)(2,1)}, bf16[1024,384]{1,0:T(8,128)(2,1)S(1)}) custom-call(s32[1,1024]{1,0:T(1,128)S(1)} %reshape.28.target_row, s32[1024,1]{1,0:T(8,128)S(1)} %copy-done.9, bf16[1024,384]{1,0:T(8,128)(2,1)S(1)} %bitcast.12), custom_call_target="tpu_custom_call" | custom-call | flops 805306368 | bytes 6291456 | tf_op jit(solution)/shard_map/select/pallas_call | solution.py:13
  35.6 0.9 copy-done.7
  36.5 0.1 copy.12
  36.5 0.0 collective-permute-done.1.east
  36.5 0.0 collective-permute-done.3.north
  36.5 0.0 collective-permute-done.west
  36.6 0.0 collective-permute-done.2.south
  36.6 1.1 %copy-done.8 = bf16[1024,384]{1,0:T(8,128)(2,1)S(1)} copy-done((bf16[1024,384]{1,0:T(8,128)(2,1)S(1)}, bf16[1024,384]{1,0:T(8,128)(2,1)}, u32[]{:S(2)}) %copy-start.8) | copy-done | bytes 786456
  37.7 1.4 %advect.1 = (f32[32,32,128]{2,1,0:T(8,128)}, bf16[1024,512]{1,0:T(8,128)(2,1)S(1)}) custom-call(f32[32,32,128]{2,1,0:T(8,128)S(1)} %copy-done.2, bf16[32,32,128]{2,1,0:T(8,128)(2,1)S(1)} %copy-done.4, bf16[32,32,128]{2,1,0:T(8,128)(2,1)S(1)} %copy-done.6, f32[32,32]{1,0:T(8,128)S(1)} %bitcast.11, f32[2,32,128]{2,1,0:T(8,128)S(1)} %collective-permute-done.west, ...), custom_call_target="tpu_custom_call" | custom-call | flops 268435456 | bytes 6291456 | tf_op jit(solution)/shard_map/advect/pallas_call | solution.py:13
  39.1 37.7 %all_to_all.10 = bf16[64,16,512]{2,1,0:T(8,128)(2,1)S(1)} all-to-all(bf16[64,16,512]{2,1,0:T(8,128)(2,1)S(1)} %bitcast.8), channel_id=1, replica_groups=mesh['face'=16,'blk'=64] {'blk'}, dimensions={0} | all-to-all | bytes 2097152 | tf_op jit(solution)/shard_map/all_to_all | solution.py:208
  76.8 5.3 %net.1 = bf16[1024,256]{1,0:T(8,128)(2,1)S(1)} custom-call(bf16[1024,512]{1,0:T(8,128)(2,1)S(1)} %bitcast.9, bf16[1,512,512]{2,1,0:T(8,128)(2,1)S(1)} %copy-done.12, bf16[1,4,512,512]{3,2,1,0:T(8,128)(2,1)S(1)} %copy-done.10, bf16[1,512,256]{2,1,0:T(8,128)(2,1)S(1)} %copy-done.13), custom_call_target="tpu_custom_call" | custom-call | flops 2952790016 | bytes 5242880 | tf_op jit(solution)/shard_map/net/pallas_call | solution.py:13
  82.2 27.7 %all_to_all.11 = bf16[64,16,256]{2,1,0:T(8,128)(2,1)S(1)} all-to-all(bf16[64,16,256]{2,1,0:T(8,128)(2,1)S(1)} %bitcast.10), channel_id=1, replica_groups=mesh['face'=16,'blk'=64] {'blk'}, dimensions={0} | all-to-all | bytes 1048576 | tf_op jit(solution)/shard_map/all_to_all | solution.py:219
  109.9 2.0 %unpack.1 = bf16[1024,256]{1,0:T(8,128)(2,1)} custom-call(bf16[1024,1024]{1,0:T(8,128)(2,1)S(1)} %copy-done, bf16[1024,256]{1,0:T(8,128)(2,1)S(1)} %bitcast.7), custom_call_target="tpu_custom_call" | custom-call | flops 536870912 | bytes 3145728 | tf_op jit(solution)/shard_map/unpack/pallas_call | solution.py:13
  (24 shorter events, 0.1 us)
Async XLA Ops:
  0.6 1.0 copy-start.1
  1.7 0.9 copy-start.3
  2.6 0.9 copy-start.5
  3.6 32.9 %copy-start.14 = (f32[32,32]{1,0:T(8,128)S(1)}, f32[32,32]{1,0:T(8,128)}, u32[]{:S(2)}) copy-start(f32[32,32]{1,0:T(8,128)} %param.12) | copy-start | bytes 12292
  3.6 33.0 %copy-start.2 = (f32[32,32,128]{2,1,0:T(8,128)S(1)}, f32[32,32,128]{2,1,0:T(8,128)}, u32[]{:S(2)}) copy-start(f32[32,32,128]{2,1,0:T(8,128)} %tracer.3) | copy-start | bytes 1572868
  3.6 33.0 %copy-start.4 = (bf16[32,32,128]{2,1,0:T(8,128)(2,1)S(1)}, bf16[32,32,128]{2,1,0:T(8,128)(2,1)}, u32[]{:S(2)}) copy-start(bf16[32,32,128]{2,1,0:T(8,128)(2,1)} %wind_x.3) | copy-start | bytes 786436
  3.6 33.0 %copy-start.6 = (bf16[32,32,128]{2,1,0:T(8,128)(2,1)S(1)}, bf16[32,32,128]{2,1,0:T(8,128)(2,1)}, u32[]{:S(2)}) copy-start(bf16[32,32,128]{2,1,0:T(8,128)(2,1)} %wind_y.3) | copy-start | bytes 786436
  3.6 32.9 %collective-permute-start.1 = (f32[32,128]{1,0:T(8,128)S(1)}, f32[32,128]{1,0:T(8,128)S(1)}, u32[]{:S(2)}, u32[]{:S(2)}) collective-permute-start(f32[32,128]{1,0:T(8,128)S(1)} %get-tuple-element.12), channel_id=1, source_target_pairs={{64,0},{128,64},{192,128},{256,192},{320,256},{384,320},{448,384},... | collective-permute-start | bytes 49160 | tf_op jit(solution)/shard_map/ppermute | solution.py:167
  4.5 32.0 %collective-permute-start.3 = (f32[32,128]{1,0:T(8,128)S(1)}, f32[32,128]{1,0:T(8,128)S(1)}, u32[]{:S(2)}, u32[]{:S(2)}) collective-permute-start(f32[32,128]{1,0:T(8,128)S(1)} %get-tuple-element.14), channel_id=1, source_target_pairs={{1,0},{2,1},{3,2},{4,3},{5,4},{6,5},{7,6},{8,7},{9,8},{10,9},{11,1... | collective-permute-start | bytes 49160 | tf_op jit(solution)/shard_map/ppermute | solution.py:170
  25.5 11.0 %collective-permute-start = (f32[2,32,128]{2,1,0:T(8,128)S(1)}, f32[2,32,128]{2,1,0:T(8,128)S(1)}, u32[]{:S(2)}, u32[]{:S(2)}) collective-permute-start(f32[2,32,128]{2,1,0:T(8,128)S(1)} %get-tuple-element.11), channel_id=1, source_target_pairs={{0,64},{64,128},{128,192},{192,256},{256,320},{320,384},{384,448},... | collective-permute-start | bytes 98312 | tf_op jit(solution)/shard_map/ppermute | solution.py:166
  25.6 11.0 %collective-permute-start.2 = (f32[2,32,128]{2,1,0:T(8,128)S(1)}, f32[2,32,128]{2,1,0:T(8,128)S(1)}, u32[]{:S(2)}, u32[]{:S(2)}) collective-permute-start(f32[2,32,128]{2,1,0:T(8,128)S(1)} %get-tuple-element.13), channel_id=1, source_target_pairs={{0,1},{1,2},{2,3},{3,4},{4,5},{5,6},{6,7},{7,8},{8,9},{9,10},{10,1... | collective-permute-start | bytes 98312 | tf_op jit(solution)/shard_map/ppermute | solution.py:169
  30.3 1.0 copy-start.9
  31.4 1.1 %copy-start.11 = (bf16[32,32,384]{2,1,0:T(8,128)(2,1)S(1)}, bf16[32,32,384]{2,1,0:T(8,128)(2,1)}, u32[]{:S(2)}) copy-start(bf16[32,32,384]{2,1,0:T(8,128)(2,1)} %param.13) | copy-start | bytes 2359300
  35.6 0.9 copy-start.7
  36.6 1.1 %copy-start.8 = (bf16[1024,384]{1,0:T(8,128)(2,1)S(1)}, bf16[1024,384]{1,0:T(8,128)(2,1)}, u32[]{:S(2)}) copy-start(bf16[1024,384]{1,0:T(8,128)(2,1)} %copy-done.7) | copy-start | bytes 2359300
  37.7 39.1 %copy-start.10 = (bf16[1,4,512,512]{3,2,1,0:T(8,128)(2,1)S(1)}, bf16[1,4,512,512]{3,2,1,0:T(8,128)(2,1)}, u32[]{:S(2)}) copy-start(bf16[1,4,512,512]{3,2,1,0:T(8,128)(2,1)} %w_hidden.1) | copy-start | bytes 6291460
  37.7 39.1 %copy-start.12 = (bf16[1,512,512]{2,1,0:T(8,128)(2,1)S(1)}, bf16[1,512,512]{2,1,0:T(8,128)(2,1)}, u32[]{:S(2)}) copy-start(bf16[1,512,512]{2,1,0:T(8,128)(2,1)} %w_in.1) | copy-start | bytes 1572868
  37.7 39.1 %copy-start.13 = (bf16[1,512,256]{2,1,0:T(8,128)(2,1)S(1)}, bf16[1,512,256]{2,1,0:T(8,128)(2,1)}, u32[]{:S(2)}) copy-start(bf16[1,512,256]{2,1,0:T(8,128)(2,1)} %w_out.1) | copy-start | bytes 786436
  76.8 33.1 %copy-start = (bf16[1024,1024]{1,0:T(8,128)(2,1)S(1)}, bf16[1024,1024]{1,0:T(8,128)(2,1)}, u32[]{:S(2)}) copy-start(bf16[1024,1024]{1,0:T(8,128)(2,1)} %get-tuple-element.18.to_columns) | copy-start | bytes 6291460

commit v2 on v1

v2 whole, which is shorter than its diff:
```python
import jax
import jax.numpy as jnp
from jax import lax
from jax.experimental import pallas as pl
from jax.experimental.pallas import tpu as pltpu
from jax.sharding import PartitionSpec as P

SLOPE = 0.15
VMEM = pl.BlockSpec(memory_space=pltpu.VMEM)


HBM = pl.BlockSpec(memory_space=pltpu.HBM)


def call(kernel, outs, operands, name, flops=0, touched=0, scratch=(), specs=None, limit=16 << 20):
    return pl.pallas_call(
        kernel,
        out_shape=outs,
        in_specs=specs or [VMEM] * len(operands),
        out_specs=jax.tree.map(lambda _: VMEM, outs),
        scratch_shapes=list(scratch),
        compiler_params=pltpu.CompilerParams(vmem_limit_bytes=limit),
        cost_estimate=pl.CostEstimate(flops=flops, bytes_accessed=touched, transcendentals=0),
        name=name,
    )(*operands)


def edges_kernel(
    tracer,
    wind_x,
    wind_y,
    last_x,
    first_x,
    last_y,
    first_y,
    low_rows,
    high_rows,
    speed_x,
    speed_y,
    arrived,
):
    cells_x, cells_y, _ = tracer.shape
    copies = [
        pltpu.make_async_copy(source, target, arrived.at[index])
        for index, (source, target) in enumerate(
            (
                (tracer.at[pl.ds(cells_x - 1, 1)], last_x.at[pl.ds(0, 1)]),
                (tracer.at[pl.ds(0, 1)], first_x),
                (wind_x.at[pl.ds(cells_x - 1, 1)], speed_x),
                (tracer.at[:, pl.ds(0, 8), :], low_rows),
                (tracer.at[:, pl.ds(cells_y - 8, 8), :], high_rows),
                (wind_y.at[:, pl.ds(cells_y - 16, 16), :], speed_y),
            )
        )
    ]
    for copy in copies:
        copy.start()
    for copy in copies:
        copy.wait()
    last_x[1] = speed_x[0].astype(jnp.float32)
    first_y[0] = low_rows[:, 0, :]
    last_y[0] = high_rows[:, 7, :]
    last_y[1] = speed_y[...].astype(jnp.float32)[:, 15, :]


def row_of(target, columns):
    cells_x, cells_y = target.shape
    lane = lax.broadcasted_iota(jnp.int32, (cells_y, columns), 1)
    place = lax.broadcasted_iota(jnp.int32, (cells_y, columns), 0)
    spread = jnp.where(lane % cells_y == place, 1.0, 0.0).astype(jnp.bfloat16)
    high = jnp.dot(
        (target >> 4).astype(jnp.float32).astype(jnp.bfloat16),
        spread,
        preferred_element_type=jnp.float32,
    )
    low = jnp.dot(
        (target & 15).astype(jnp.float32).astype(jnp.bfloat16),
        spread,
        preferred_element_type=jnp.float32,
    )
    lane = lax.broadcasted_iota(jnp.int32, (cells_x, columns), 1)
    place = lax.broadcasted_iota(jnp.int32, (cells_x, columns), 0)
    own = jnp.where(lane // cells_y == place, 16.0 * high + low, 0.0)
    return jnp.sum(own, axis=0, keepdims=True).astype(jnp.int32)


def select_kernel(target, forcing, to_slots, packed, rows, arrived):
    copy = pltpu.make_async_copy(forcing, rows, arrived)
    copy.start()
    slots, columns = to_slots.shape
    step = 128
    row = row_of(target[...], columns)

    def body(index, _):
        chunk = pl.ds(pl.multiple_of(index * step, step), step)
        place = lax.broadcasted_iota(jnp.int32, (step, columns), 0) + index * step
        to_slots[chunk, :] = jnp.where(row == place, 1.0, 0.0).astype(jnp.bfloat16)
        return 0

    lax.fori_loop(0, slots // step, body, 0)
    copy.wait()
    packed[...] = jnp.dot(
        to_slots[...], rows[...], preferred_element_type=jnp.float32
    ).astype(jnp.bfloat16)


def advect_kernel(
    tracer,
    wind_x,
    wind_y,
    area,
    west,
    east,
    south,
    north,
    to_slots,
    packed_forcing,
    advected,
    features,
    rounded,
):
    cells_x, cells_y, levels = tracer.shape
    inverse = jnp.transpose(1.0 / area[...])
    place = lax.broadcasted_iota(jnp.int32, (cells_y, levels), 0)
    west_speed = west[1]
    flux_before = jnp.maximum(west_speed, 0.0) * west[0] + jnp.minimum(west_speed, 0.0) * tracer[0]
    for i in range(cells_x):
        here = tracer[i]
        after = tracer[i + 1] if i + 1 < cells_x else east[0]
        speed = wind_x[i].astype(jnp.float32)
        flux_x = jnp.maximum(speed, 0.0) * here + jnp.minimum(speed, 0.0) * after
        speed = wind_y[i].astype(jnp.float32)
        beyond = jnp.where(
            place == cells_y - 1, north[0, i : i + 1, :], pltpu.roll(here, cells_y - 1, 0)
        )
        flux_y = jnp.maximum(speed, 0.0) * here + jnp.minimum(speed, 0.0) * beyond
        south_speed = south[1, i : i + 1, :]
        south_flux = (
            jnp.maximum(south_speed, 0.0) * south[0, i : i + 1, :]
            + jnp.minimum(south_speed, 0.0) * here[0:1, :]
        )
        flux_y_before = jnp.where(place == 0, south_flux, pltpu.roll(flux_y, 1, 0))
        spread = (flux_x - flux_before) + (flux_y - flux_y_before)
        moved = here - spread * inverse[:, i : i + 1]
        advected[i] = moved
        rounded[i * cells_y : (i + 1) * cells_y, :] = moved.astype(jnp.bfloat16)
        flux_before = flux_x
    features[:, levels:] = packed_forcing[...]
    features[:, :levels] = jnp.dot(
        to_slots[...], rounded[...], preferred_element_type=jnp.float32
    ).astype(jnp.bfloat16)


def net_kernel(rows_in, w_in, w_hidden, w_out, result, ping, pong):
    step = 256

    def leaky(values):
        return jnp.maximum(values, SLOPE * values)

    def layer(source, weights, target, finish):
        for start in range(0, source.shape[0], step):
            rows = slice(start, start + step)
            sums = jnp.dot(source[rows, :], weights, preferred_element_type=jnp.float32)
            target[rows, :] = finish(sums).astype(jnp.bfloat16)

    layer(rows_in, w_in[0], ping, leaky)
    here, there = ping, pong
    for index in range(w_hidden.shape[1]):
        layer(here, w_hidden[0, index], there, leaky)
        here, there = there, here
    layer(here, w_out[0], result, lambda sums: sums)


def unpack_kernel(target, returned, tendencies, to_columns):
    cells_x, cells_y = target.shape
    slots = returned.shape[0]
    turned = jnp.transpose(target[...].astype(jnp.float32)).astype(jnp.int32)
    place = lax.broadcasted_iota(jnp.int32, (cells_y, slots), 1)
    per = 8
    for first in range(0, cells_x, per):
        for i in range(first, first + per):
            to_columns[i * cells_y : (i + 1) * cells_y, :] = jnp.where(
                turned[:, i : i + 1] == place, 1.0, 0.0
            ).astype(jnp.bfloat16)
        rows = slice(first * cells_y, (first + per) * cells_y)
        tendencies[rows, :] = jnp.dot(
            to_columns[rows, :], returned[...], preferred_element_type=jnp.float32
        ).astype(jnp.bfloat16)


def neighbours(axis):
    count = lax.axis_size(axis)
    forward = [(i, (i + 1) % count) for i in range(count)]
    return forward, [(target, source) for source, target in forward]


def local(tracer, wind_x, wind_y, cell_area, forcing, group_map, w_in, w_hidden, w_out):
    groups = lax.axis_size("blk")
    cells_x, cells_y, levels = tracer.shape
    columns = cells_x * cells_y
    slots_per = columns // groups
    width = levels + forcing.shape[2]
    width_out = w_out.shape[2]
    f32, bf16 = jnp.float32, jnp.bfloat16
    shaped = jax.ShapeDtypeStruct

    last_x, first_x, last_y, first_y = call(
        edges_kernel,
        [
            shaped((2, cells_y, levels), f32),
            shaped((1, cells_y, levels), f32),
            shaped((2, cells_x, levels), f32),
            shaped((1, cells_x, levels), f32),
        ],
        [tracer, wind_x, wind_y],
        "edges",
        touched=1 << 19,
        scratch=[
            pltpu.VMEM((cells_x, 8, levels), f32),
            pltpu.VMEM((cells_x, 8, levels), f32),
            pltpu.VMEM((1, cells_y, levels), bf16),
            pltpu.VMEM((cells_x, 16, levels), bf16),
            pltpu.SemaphoreType.DMA((6,)),
        ],
        specs=[HBM] * 3,
        limit=60 << 20,
    )
    forward, backward = neighbours("face")
    west = lax.ppermute(last_x, "face", forward)
    east = lax.ppermute(first_x, "face", backward)
    forward, backward = neighbours("blk")
    south = lax.ppermute(last_y, "blk", forward)
    north = lax.ppermute(first_y, "blk", backward)

    to_slots, packed_forcing = call(
        select_kernel,
        [shaped((columns, columns), bf16), shaped((columns, forcing.shape[2]), bf16)],
        [group_map, forcing.reshape(columns, forcing.shape[2])],
        "select",
        flops=2 * columns * columns * forcing.shape[2],
        touched=4 << 20,
        scratch=[pltpu.VMEM((columns, forcing.shape[2]), bf16), pltpu.SemaphoreType.DMA],
        specs=[VMEM, HBM],
    )
    advected, features = call(
        advect_kernel,
        [shaped(tracer.shape, f32), shaped((columns, width), bf16)],
        [tracer, wind_x, wind_y, cell_area, west, east, south, north, to_slots, packed_forcing],
        "advect",
        flops=2 * columns * columns * levels,
        touched=6 << 20,
        scratch=[pltpu.VMEM((columns, levels), bf16)],
    )
    received = lax.all_to_all(
        features.reshape(groups, slots_per, width), "blk", split_axis=0, concat_axis=0, tiled=True
    )
    result = call(
        net_kernel,
        shaped((columns, width_out), bf16),
        [received.reshape(columns, width), w_in, w_hidden, w_out],
        "net",
        flops=2 * columns * (w_in.size + w_hidden.size + w_out.size),
        touched=5 << 20,
        scratch=[pltpu.VMEM((columns, w_in.shape[2]), bf16)] * 2,
    )
    returned = lax.all_to_all(
        result.reshape(groups, slots_per, width_out), "blk", split_axis=0, concat_axis=0, tiled=True
    )
    tendencies = call(
        unpack_kernel,
        shaped((columns, width_out), bf16),
        [group_map, returned.reshape(columns, width_out)],
        "unpack",
        flops=2 * columns * columns * width_out,
        touched=1 << 20,
        scratch=[pltpu.VMEM((columns, columns), bf16)],
    )
    return advected, tendencies.reshape(cells_x, cells_y, width_out)


def solution(mesh):
    placed = (
        P("face", "blk", None),
        P("face", "blk", None),
        P("face", "blk", None),
        P("face", "blk"),
        P("face", "blk", None),
        P("face", "blk"),
        P("blk", None, None),
        P("blk", None, None, None),
        P("blk", None, None),
    )
    return jax.shard_map(
        local,
        mesh=mesh,
        in_specs=placed,
        out_specs=(P("face", "blk", None), P("face", "blk", None)),
        check_vma=False,
    )
```

time: 113 us -> 102 us (0.903)
  local copies, waits for them, and re-layouts: 10.1 us -> 1.89 us
  waiting for transfers between devices: 0.01 us -> 3.66 us
  blocking collectives: 65.4 us -> 61.8 us
  Pallas kernels: 11.8 us -> 10 us
    unnamed x31 -> x20, local copies, waits for them, and re-layouts: 7.22 us -> 1.89 us
    all_to_all x1, blocking collectives: 37.7 us -> 34 us  [local(): lax.all_to_all(features.reshape(groups, slots_per, width), 'blk', split_a...]
    ppermute x1, waiting for transfers between devices: 0.01 us -> 3.65 us  [local(): south = lax.ppermute(last_y, 'blk', forward)]
    reshape x2 -> x0, local copies, waits for them, and re-layouts: 2.85 us -> none  [the longest x1 2.05 us: local(): group_map.reshape(columns, 1)]
    pallas_call x5, Pallas kernels: 11.8 us -> 10 us  [call(): pl.pallas_call(kernel, out_shape=outs, in_specs=specs or [VMEM] * len(ope...]
  transfers between devices with their start and end apart: 4 -> 4, of which waited for: 0 -> 1; matrix products, arithmetic and copies ran while one was open for 3% -> 0% of each run, Pallas kernels for 3% -> 2%
where the time goes in v2:
time: 102 us
  blocking collectives  61.8 us (61%)
  starting transfers between devices  23.8 us (23%)
  Pallas kernels  10 us (10%)
  waiting for transfers between devices  3.66 us (4%)
  local copies, waits for them, and re-layouts  1.89 us (2%)
    all_to_all x1, blocking collectives, local(): lax.all_to_all(features.reshape(groups, slots_per, width), 'blk', split_a...  34 us
    all_to_all x1, blocking collectives, local(): lax.all_to_all(result.reshape(groups, slots_per, width_out), 'blk', split...  27.8 us
    ppermute x1, starting transfers between devices, local(): north = lax.ppermute(first_y, 'blk', backward)  21 us
    pallas_call x5, Pallas kernels, call(): pl.pallas_call(kernel, out_shape=outs, in_specs=specs or [VMEM] * len(ope...  10 us
    ppermute x1, waiting for transfers between devices, local(): south = lax.ppermute(last_y, 'blk', forward)  3.65 us
  transfers between devices with their start and end apart: 4, of which 1 were waited for; matrix products, arithmetic and copies ran while one was open for 0% of the time, Pallas kernels for 2%

profile of v2, /device:TPU:14, one launch (start us, length us, event | category | flops | bytes accessed | tf_op | source)
XLA Modules:
  0.0 101.9 jit_solution(5070281659535635525)
XLA Ops:
  0.7 1.9 %edges.1 = (f32[2,32,128]{2,1,0:T(8,128)}, f32[1,32,128]{2,1,0:T(8,128)}, f32[2,32,128]{2,1,0:T(8,128)}, f32[1,32,128]{2,1,0:T(8,128)}) custom-call(f32[32,32,128]{2,1,0:T(8,128)} %tracer.3, bf16[32,32,128]{2,1,0:T(8,128)(2,1)} %wind_x.3, bf16[32,32,128]{2,1,0:T(8,128)(2,1)} %wind_y.3), custom_call_target="tpu_custom_call" | custom-call | bytes 524288 | tf_op jit(solution)/shard_map/edges/pallas_call | solution.py:16
  2.5 0.9 collective-permute-start.1
  3.4 21.0 %collective-permute-start.3 = (f32[1,32,128]{2,1,0:T(8,128)}, f32[1,32,128]{2,1,0:T(8,128)S(1)}, u32[]{:S(2)}, u32[]{:S(2)}) collective-permute-start(f32[1,32,128]{2,1,0:T(8,128)} %get-tuple-element.13), channel_id=1, source_target_pairs={{1,0},{2,1},{3,2},{4,3},{5,4},{6,5},{7,6},{8,7},{9,8},{10,9},{11,1... | collective-permute-start | bytes 49160 | tf_op jit(solution)/shard_map/ppermute | solution.py:233
  24.4 0.0 collective-permute-start
  24.5 1.9 %collective-permute-start.2 = (f32[2,32,128]{2,1,0:T(8,128)}, f32[2,32,128]{2,1,0:T(8,128)S(1)}, u32[]{:S(2)}, u32[]{:S(2)}) collective-permute-start(f32[2,32,128]{2,1,0:T(8,128)} %get-tuple-element.12), channel_id=1, source_target_pairs={{0,1},{1,2},{2,3},{3,4},{4,5},{5,6},{6,7},{7,8},{8,9},{9,10},{10,1... | collective-permute-start | bytes 98312 | tf_op jit(solution)/shard_map/ppermute | solution.py:232
  26.4 0.0 copy-start.5
  26.4 1.1 %copy-done.5 = bf16[32,32,384]{2,1,0:T(8,128)(2,1)S(1)} copy-done((bf16[32,32,384]{2,1,0:T(8,128)(2,1)S(1)}, bf16[32,32,384]{2,1,0:T(8,128)(2,1)}, u32[]{:S(2)}) %copy-start.5) | copy-done | bytes 786456
  27.5 0.7 copy-done.8
  28.2 1.9 %select.1 = (bf16[1024,1024]{1,0:T(8,128)(2,1)S(1)}, bf16[1024,384]{1,0:T(8,128)(2,1)S(1)}) custom-call(s32[32,32]{1,0:T(8,128)S(1)} %copy-done.8, bf16[1024,384]{1,0:T(8,128)(2,1)S(1)} %bitcast.10), custom_call_target="tpu_custom_call" | custom-call | flops 805306368 | bytes 4194304 | tf_op jit(solution)/shard_map/select/pallas_call | solution.py:16
  30.1 0.0 collective-permute-done.1.east
  30.1 0.0 collective-permute-done.3.north
  30.1 0.0 collective-permute-done.west
  30.2 3.6 %collective-permute-done.2.south = f32[2,32,128]{2,1,0:T(8,128)S(1)} collective-permute-done((f32[2,32,128]{2,1,0:T(8,128)}, f32[2,32,128]{2,1,0:T(8,128)S(1)}, u32[]{:S(2)}, u32[]{:S(2)}) %collective-permute-start.2) | collective-permute-done | bytes 32800 | tf_op jit(solution)/shard_map/ppermute | solution.py:232
  33.8 0.0 copy-done.2
  33.8 0.0 copy-start.4
  33.8 0.0 copy-start.6
  33.9 0.0 copy-start.7
  33.9 1.4 %advect.1 = (f32[32,32,128]{2,1,0:T(8,128)}, bf16[1024,512]{1,0:T(8,128)(2,1)S(1)}) custom-call(f32[32,32,128]{2,1,0:T(8,128)S(1)} %copy-done, bf16[32,32,128]{2,1,0:T(8,128)(2,1)S(1)} %copy-done.1, bf16[32,32,128]{2,1,0:T(8,128)(2,1)S(1)} %copy-done.2, f32[32,32]{1,0:T(8,128)S(1)} %copy-done.3, f32[2,32,128]{2,1,0:T(8,128)S(1)} %collective-permute-done.west, ...), custom_call_target="tpu_custom_call" | custom-call | flops 268435456 | bytes 6291456 | tf_op jit(solution)/shard_map/advect/pallas_call | solution.py:16
  35.3 34.0 %all_to_all.10 = bf16[64,16,512]{2,1,0:T(8,128)(2,1)S(1)} all-to-all(bf16[64,16,512]{2,1,0:T(8,128)(2,1)S(1)} %bitcast.6), channel_id=1, replica_groups=mesh['face'=16,'blk'=64] {'blk'}, dimensions={0} | all-to-all | bytes 2097152 | tf_op jit(solution)/shard_map/all_to_all | solution.py:254
  69.3 0.0 copy-done.6
  69.3 0.0 copy-start.9
  69.3 3.2 %net.1 = bf16[1024,256]{1,0:T(8,128)(2,1)S(1)} custom-call(bf16[1024,512]{1,0:T(8,128)(2,1)S(1)} %bitcast.7, bf16[1,512,512]{2,1,0:T(8,128)(2,1)S(1)} %copy-done.6, bf16[1,4,512,512]{3,2,1,0:T(8,128)(2,1)S(1)} %copy-done.4, bf16[1,512,256]{2,1,0:T(8,128)(2,1)S(1)} %copy-done.7), custom_call_target="tpu_custom_call" | custom-call | flops 2952790016 | bytes 5242880 | tf_op jit(solution)/shard_map/net/pallas_call | solution.py:16
  72.5 27.8 %all_to_all.11 = bf16[64,16,256]{2,1,0:T(8,128)(2,1)S(1)} all-to-all(bf16[64,16,256]{2,1,0:T(8,128)(2,1)S(1)} %bitcast.8), channel_id=1, replica_groups=mesh['face'=16,'blk'=64] {'blk'}, dimensions={0} | all-to-all | bytes 1048576 | tf_op jit(solution)/shard_map/all_to_all | solution.py:266
  100.3 1.7 %unpack.1 = bf16[1024,256]{1,0:T(8,128)(2,1)} custom-call(s32[32,32]{1,0:T(8,128)S(1)} %copy-done.9, bf16[1024,256]{1,0:T(8,128)(2,1)S(1)} %bitcast.9), custom_call_target="tpu_custom_call" | custom-call | flops 536870912 | bytes 1048576 | tf_op jit(solution)/shard_map/unpack/pallas_call | solution.py:16
  (11 shorter events, 0.0 us)
Async XLA Ops:
  0.6 33.2 %copy-start.2 = (bf16[32,32,128]{2,1,0:T(8,128)(2,1)S(1)}, bf16[32,32,128]{2,1,0:T(8,128)(2,1)}, u32[]{:S(2)}) copy-start(bf16[32,32,128]{2,1,0:T(8,128)(2,1)} %wind_y.3) | copy-start | bytes 786436
  0.6 33.2 %copy-start.1 = (bf16[32,32,128]{2,1,0:T(8,128)(2,1)S(1)}, bf16[32,32,128]{2,1,0:T(8,128)(2,1)}, u32[]{:S(2)}) copy-start(bf16[32,32,128]{2,1,0:T(8,128)(2,1)} %wind_x.3) | copy-start | bytes 786436
  0.7 33.2 %copy-start = (f32[32,32,128]{2,1,0:T(8,128)S(1)}, f32[32,32,128]{2,1,0:T(8,128)}, u32[]{:S(2)}) copy-start(f32[32,32,128]{2,1,0:T(8,128)} %tracer.3) | copy-start | bytes 1572868
  0.7 33.2 %copy-start.3 = (f32[32,32]{1,0:T(8,128)S(1)}, f32[32,32]{1,0:T(8,128)}, u32[]{:S(2)}) copy-start(f32[32,32]{1,0:T(8,128)} %area.1) | copy-start | bytes 12292
  2.5 27.6 %collective-permute-start.1 = (f32[1,32,128]{2,1,0:T(8,128)}, f32[1,32,128]{2,1,0:T(8,128)S(1)}, u32[]{:S(2)}, u32[]{:S(2)}) collective-permute-start(f32[1,32,128]{2,1,0:T(8,128)} %get-tuple-element.11), channel_id=1, source_target_pairs={{64,0},{128,64},{192,128},{256,192},{320,256},{384,320},{448,384},... | collective-permute-start | bytes 49160 | tf_op jit(solution)/shard_map/ppermute | solution.py:230
  3.4 26.7 %collective-permute-start.3 = (f32[1,32,128]{2,1,0:T(8,128)}, f32[1,32,128]{2,1,0:T(8,128)S(1)}, u32[]{:S(2)}, u32[]{:S(2)}) collective-permute-start(f32[1,32,128]{2,1,0:T(8,128)} %get-tuple-element.13), channel_id=1, source_target_pairs={{1,0},{2,1},{3,2},{4,3},{5,4},{6,5},{7,6},{8,7},{9,8},{10,9},{11,1... | collective-permute-start | bytes 49160 | tf_op jit(solution)/shard_map/ppermute | solution.py:233
  24.4 5.7 %collective-permute-start = (f32[2,32,128]{2,1,0:T(8,128)}, f32[2,32,128]{2,1,0:T(8,128)S(1)}, u32[]{:S(2)}, u32[]{:S(2)}) collective-permute-start(f32[2,32,128]{2,1,0:T(8,128)} %get-tuple-element.10), channel_id=1, source_target_pairs={{0,64},{64,128},{128,192},{192,256},{256,320},{320,384},{384,448},... | collective-permute-start | bytes 98312 | tf_op jit(solution)/shard_map/ppermute | solution.py:229
  24.5 9.3 %collective-permute-start.2 = (f32[2,32,128]{2,1,0:T(8,128)}, f32[2,32,128]{2,1,0:T(8,128)S(1)}, u32[]{:S(2)}, u32[]{:S(2)}) collective-permute-start(f32[2,32,128]{2,1,0:T(8,128)} %get-tuple-element.12), channel_id=1, source_target_pairs={{0,1},{1,2},{2,3},{3,4},{4,5},{5,6},{6,7},{7,8},{8,9},{9,10},{10,1... | collective-permute-start | bytes 98312 | tf_op jit(solution)/shard_map/ppermute | solution.py:232
  26.4 1.1 %copy-start.5 = (bf16[32,32,384]{2,1,0:T(8,128)(2,1)S(1)}, bf16[32,32,384]{2,1,0:T(8,128)(2,1)}, u32[]{:S(2)}) copy-start(bf16[32,32,384]{2,1,0:T(8,128)(2,1)} %param.13) | copy-start | bytes 2359300
  27.5 0.7 copy-start.8
  33.8 35.4 %copy-start.4 = (bf16[1,4,512,512]{3,2,1,0:T(8,128)(2,1)S(1)}, bf16[1,4,512,512]{3,2,1,0:T(8,128)(2,1)}, u32[]{:S(2)}) copy-start(bf16[1,4,512,512]{3,2,1,0:T(8,128)(2,1)} %w_hidden.1) | copy-start | bytes 6291460
  33.8 35.4 %copy-start.6 = (bf16[1,512,512]{2,1,0:T(8,128)(2,1)S(1)}, bf16[1,512,512]{2,1,0:T(8,128)(2,1)}, u32[]{:S(2)}) copy-start(bf16[1,512,512]{2,1,0:T(8,128)(2,1)} %w_in.1) | copy-start | bytes 1572868
  33.9 35.4 %copy-start.7 = (bf16[1,512,256]{2,1,0:T(8,128)(2,1)S(1)}, bf16[1,512,256]{2,1,0:T(8,128)(2,1)}, u32[]{:S(2)}) copy-start(bf16[1,512,256]{2,1,0:T(8,128)(2,1)} %w_out.1) | copy-start | bytes 786436
  69.3 31.0 %copy-start.9 = (s32[32,32]{1,0:T(8,128)S(1)}, s32[32,32]{1,0:T(8,128)}, u32[]{:S(2)}) copy-start(s32[32,32]{1,0:T(8,128)} %target.3) | copy-start | bytes 12292

commit v3 on v2

--- a/solution.py
+++ b/solution.py
@@ -12,27 +12,33 @@
 HBM = pl.BlockSpec(memory_space=pltpu.HBM)
 
 
-def call(kernel, outs, operands, name, flops=0, touched=0, scratch=(), specs=None, limit=16 << 20):
+def call(kernel, outs, operands, name, flops=0, touched=0, scratch=(), specs=None, out_specs=None):
     return pl.pallas_call(
         kernel,
         out_shape=outs,
         in_specs=specs or [VMEM] * len(operands),
-        out_specs=jax.tree.map(lambda _: VMEM, outs),
+        out_specs=out_specs or jax.tree.map(lambda _: VMEM, outs),
         scratch_shapes=list(scratch),
-        compiler_params=pltpu.CompilerParams(vmem_limit_bytes=limit),
+        compiler_params=pltpu.CompilerParams(vmem_limit_bytes=16 << 20),
         cost_estimate=pl.CostEstimate(flops=flops, bytes_accessed=touched, transcendentals=0),
         name=name,
     )(*operands)
+
+
+def in_hbm(array):
+    return pltpu.with_memory_space_constraint(array, pltpu.HBM)
 
 
 def edges_kernel(
     tracer,
     wind_x,
     wind_y,
+    target,
     last_x,
     first_x,
     last_y,
     first_y,
+    held_target,
     low_rows,
     high_rows,
     speed_x,
@@ -45,16 +51,19 @@
         for index, (source, target) in enumerate(
             (
                 (tracer.at[pl.ds(cells_x - 1, 1)], last_x.at[pl.ds(0, 1)]),
-                (tracer.at[pl.ds(0, 1)], first_x),
+                (tracer.at[pl.ds(0, 1)], first_x.at[pl.ds(0, 1)]),
                 (wind_x.at[pl.ds(cells_x - 1, 1)], speed_x),
                 (tracer.at[:, pl.ds(0, 8), :], low_rows),
                 (tracer.at[:, pl.ds(cells_y - 8, 8), :], high_rows),
                 (wind_y.at[:, pl.ds(cells_y - 16, 16), :], speed_y),
+                (target, held_target),
             )
         )
     ]
     for copy in copies:
         copy.start()
+    first_x[1] = jnp.zeros(first_x.shape[1:], jnp.float32)
+    first_y[1] = jnp.zeros(first_y.shape[1:], jnp.float32)
     for copy in copies:
         copy.wait()
     last_x[1] = speed_x[0].astype(jnp.float32)
@@ -109,10 +118,10 @@
     wind_x,
     wind_y,
     area,
+    south,
+    north,
     west,
     east,
-    south,
-    north,
     to_slots,
     packed_forcing,
     advected,
@@ -151,8 +160,12 @@
     ).astype(jnp.bfloat16)
 
 
-def net_kernel(rows_in, w_in, w_hidden, w_out, result, ping, pong):
+def net_kernel(
+    rows_in, w_in, w_hidden, w_out, advected, result, advected_out, ping, pong, stored
+):
     step = 256
+    copy = pltpu.make_async_copy(advected, advected_out, stored)
+    copy.start()
 
     def leaky(values):
         return jnp.maximum(values, SLOPE * values)
@@ -169,6 +182,7 @@
         layer(here, w_hidden[0, index], there, leaky)
         here, there = there, here
     layer(here, w_out[0], result, lambda sums: sums)
+    copy.wait()
 
 
 def unpack_kernel(target, returned, tendencies, to_columns):
@@ -202,17 +216,19 @@
     width = levels + forcing.shape[2]
     width_out = w_out.shape[2]
     f32, bf16 = jnp.float32, jnp.bfloat16
-    shaped = jax.ShapeDtypeStruct
-
-    last_x, first_x, last_y, first_y = call(
+    shaped = pltpu.VMEM
+    result_of = jax.ShapeDtypeStruct
+
+    last_x, first_x, last_y, first_y, target = call(
         edges_kernel,
         [
             shaped((2, cells_y, levels), f32),
-            shaped((1, cells_y, levels), f32),
+            shaped((2, cells_y, levels), f32),
             shaped((2, cells_x, levels), f32),
-            shaped((1, cells_x, levels), f32),
+            shaped((2, cells_x, levels), f32),
+            shaped(group_map.shape, group_map.dtype),
         ],
-        [tracer, wind_x, wind_y],
+        [in_hbm(tracer), in_hbm(wind_x), in_hbm(wind_y), in_hbm(group_map)],
         "edges",
         touched=1 << 19,
         scratch=[
@@ -220,10 +236,9 @@
             pltpu.VMEM((cells_x, 8, levels), f32),
             pltpu.VMEM((1, cells_y, levels), bf16),
             pltpu.VMEM((cells_x, 16, levels), bf16),
-            pltpu.SemaphoreType.DMA((6,)),
+            pltpu.SemaphoreType.DMA((7,)),
         ],
-        specs=[HBM] * 3,
-        limit=60 << 20,
+        specs=[HBM] * 4,
     )
     forward, backward = neighbours("face")
     west = lax.ppermute(last_x, "face", forward)
@@ -235,7 +250,7 @@
     to_slots, packed_forcing = call(
         select_kernel,
         [shaped((columns, columns), bf16), shaped((columns, forcing.shape[2]), bf16)],
-        [group_map, forcing.reshape(columns, forcing.shape[2])],
+        [target, in_hbm(forcing.reshape(columns, forcing.shape[2]))],
         "select",
         flops=2 * columns * columns * forcing.shape[2],
         touched=4 << 20,
@@ -245,7 +260,7 @@
     advected, features = call(
         advect_kernel,
         [shaped(tracer.shape, f32), shaped((columns, width), bf16)],
-        [tracer, wind_x, wind_y, cell_area, west, east, south, north, to_slots, packed_forcing],
+        [tracer, wind_x, wind_y, cell_area, south, north, west, east, to_slots, packed_forcing],
         "advect",
         flops=2 * columns * columns * levels,
         touched=6 << 20,
@@ -254,22 +269,23 @@
     received = lax.all_to_all(
         features.reshape(groups, slots_per, width), "blk", split_axis=0, concat_axis=0, tiled=True
     )
-    result = call(
+    result, advected = call(
         net_kernel,
-        shaped((columns, width_out), bf16),
-        [received.reshape(columns, width), w_in, w_hidden, w_out],
+        [shaped((columns, width_out), bf16), result_of(tracer.shape, f32)],
+        [received.reshape(columns, width), w_in, w_hidden, w_out, advected],
         "net",
         flops=2 * columns * (w_in.size + w_hidden.size + w_out.size),
         touched=5 << 20,
-        scratch=[pltpu.VMEM((columns, w_in.shape[2]), bf16)] * 2,
+        scratch=[pltpu.VMEM((columns, w_in.shape[2]), bf16)] * 2 + [pltpu.SemaphoreType.DMA],
+        out_specs=[VMEM, HBM],
     )
     returned = lax.all_to_all(
         result.reshape(groups, slots_per, width_out), "blk", split_axis=0, concat_axis=0, tiled=True
     )
     tendencies = call(
         unpack_kernel,
-        shaped((columns, width_out), bf16),
-        [group_map, returned.reshape(columns, width_out)],
+        result_of((columns, width_out), bf16),
+        [target, returned.reshape(columns, width_out)],
         "unpack",
         flops=2 * columns * columns * width_out,
         touched=1 << 20,

time: 102 us -> 100 us (0.980)
  waiting for transfers between devices: 3.66 us -> 0.01 us
  blocking collectives: 61.8 us -> 64.4 us
  local copies, waits for them, and re-layouts: 1.89 us -> 0.04 us
    all_to_all x1, blocking collectives: 34 us -> 38.1 us  [local(): lax.all_to_all(features.reshape(groups, slots_per, width), 'blk', split_a...]
    ppermute x1, waiting for transfers between devices: 3.65 us -> 0.01 us  [local(): south = lax.ppermute(last_y, 'blk', forward)]
    unnamed x20 -> x14, local copies, waits for them, and re-layouts: 1.89 us -> 0.04 us
    ppermute x1, starting transfers between devices: 1.92 us -> 3.6 us  [local(): south = lax.ppermute(last_y, 'blk', forward)]
    ppermute x1, starting transfers between devices: 21 us -> 19.3 us  [local(): north = lax.ppermute(first_y, 'blk', backward)]
    all_to_all x1, blocking collectives: 27.8 us -> 26.4 us  [local(): lax.all_to_all(result.reshape(groups, slots_per, width_out), 'blk', split...]
  transfers between devices with their start and end apart: 4 -> 4, of which waited for: 1 -> 0; matrix products, arithmetic and copies ran while one was open for 0% -> 0% of each run, Pallas kernels for 2% -> 2%
where the time goes in v3:
time: 100 us; the launch traced here: 99.8 us
  blocking collectives  64.4 us (64%)
  starting transfers between devices  24.7 us (25%)
  Pallas kernels  9.77 us (10%)
    all_to_all x1, blocking collectives, local(): lax.all_to_all(features.reshape(groups, slots_per, width), 'blk', split_a...  38.1 us
    all_to_all x1, blocking collectives, local(): lax.all_to_all(result.reshape(groups, slots_per, width_out), 'blk', split...  26.4 us
    ppermute x1, starting transfers between devices, local(): north = lax.ppermute(first_y, 'blk', backward)  19.3 us
    pallas_call x5, Pallas kernels, call(): pl.pallas_call(kernel, out_shape=outs, in_specs=specs or [VMEM] * len(ope...  9.77 us
    ppermute x1, starting transfers between devices, local(): south = lax.ppermute(last_y, 'blk', forward)  3.6 us
  transfers between devices with their start and end apart: 4, of which 0 were waited for; matrix products, arithmetic and copies ran while one was open for 0% of the time, Pallas kernels for 2%

profile of v3, /device:TPU:14, one launch (start us, length us, event | category | flops | bytes accessed | tf_op | source)
XLA Modules:
  0.0 99.8 jit_solution(11837570882898124725)
XLA Ops:
  0.6 0.0 copy-start.2
  0.6 0.0 copy-start.1
  0.7 0.0 copy-start
  0.7 0.0 copy-start.3
  0.7 1.3 %edges.1 = (f32[2,32,128]{2,1,0:T(8,128)S(1)}, f32[2,32,128]{2,1,0:T(8,128)S(1)}, f32[2,32,128]{2,1,0:T(8,128)S(1)}, f32[2,32,128]{2,1,0:T(8,128)S(1)}, s32[32,32]{1,0:T(8,128)S(1)}) custom-call(f32[32,32,128]{2,1,0:T(8,128)} %tracer.3, bf16[32,32,128]{2,1,0:T(8,128)(2,1)} %wind_x.3, bf16[32,32,128]{2,1,0:T(8,128)(2,1)} %wind_y.3, s32[32,32]{1,0:T(8,128)} %target.1), custom_call_target="tpu_custom_call" | custom-call | bytes 524288 | tf_op jit(solution)/shard_map/edges/pallas_call | solution.py:16
  1.9 3.6 %collective-permute-start = (f32[2,32,128]{2,1,0:T(8,128)S(1)}, f32[2,32,128]{2,1,0:T(8,128)S(1)}, u32[]{:S(2)}, u32[]{:S(2)}) collective-permute-start(f32[2,32,128]{2,1,0:T(8,128)S(1)} %get-tuple-element.13), channel_id=1, source_target_pairs={{0,1},{1,2},{2,3},{3,4},{4,5},{5,6},{6,7},{7,8},{8,9},{9,10},{10,1... | collective-permute-start | bytes 98312 | tf_op jit(solution)/shard_map/ppermute | solution.py:247
  5.5 19.3 %collective-permute-start.1 = (f32[2,32,128]{2,1,0:T(8,128)S(1)}, f32[2,32,128]{2,1,0:T(8,128)S(1)}, u32[]{:S(2)}, u32[]{:S(2)}) collective-permute-start(f32[2,32,128]{2,1,0:T(8,128)S(1)} %get-tuple-element.14), channel_id=1, source_target_pairs={{1,0},{2,1},{3,2},{4,3},{5,4},{6,5},{7,6},{8,7},{9,8},{10,9},{11,1... | collective-permute-start | bytes 98312 | tf_op jit(solution)/shard_map/ppermute | solution.py:248
  24.9 0.0 collective-permute-start.2
  24.9 1.7 %collective-permute-start.3 = (f32[2,32,128]{2,1,0:T(8,128)S(1)}, f32[2,32,128]{2,1,0:T(8,128)S(1)}, u32[]{:S(2)}, u32[]{:S(2)}) collective-permute-start(f32[2,32,128]{2,1,0:T(8,128)S(1)} %get-tuple-element.16), channel_id=1, source_target_pairs={{64,0},{128,64},{192,128},{256,192},{320,256},{384,320},{448,384},... | collective-permute-start | bytes 98312 | tf_op jit(solution)/shard_map/ppermute | solution.py:245
  26.7 2.4 %select.1 = (bf16[1024,1024]{1,0:T(8,128)(2,1)S(1)}, bf16[1024,384]{1,0:T(8,128)(2,1)S(1)}) custom-call(s32[32,32]{1,0:T(8,128)S(1)} %get-tuple-element.17.target, bf16[1024,384]{1,0:T(8,128)(2,1)} %bitcast.10), custom_call_target="tpu_custom_call" | custom-call | flops 805306368 | bytes 4194304 | tf_op jit(solution)/shard_map/select/pallas_call | solution.py:16
  29.0 0.0 collective-permute-done.south
  29.1 0.0 collective-permute-done.1.north
  29.1 0.0 collective-permute-done.2.west
  29.1 0.0 collective-permute-done.3.east
  29.1 0.0 copy-done.2
  29.1 0.0 copy-done.1
  29.1 0.0 copy-start.4
  29.1 0.0 copy-start.5
  29.2 0.0 copy-start.6
  29.2 1.3 %advect.1 = (f32[32,32,128]{2,1,0:T(8,128)S(1)}, bf16[1024,512]{1,0:T(8,128)(2,1)S(1)}) custom-call(f32[32,32,128]{2,1,0:T(8,128)S(1)} %copy-done, bf16[32,32,128]{2,1,0:T(8,128)(2,1)S(1)} %copy-done.1, bf16[32,32,128]{2,1,0:T(8,128)(2,1)S(1)} %copy-done.2, f32[32,32]{1,0:T(8,128)S(1)} %copy-done.3, f32[2,32,128]{2,1,0:T(8,128)S(1)} %collective-permute-done.south, ...), custom_call_target="tpu_custom_call" | custom-call | flops 268435456 | bytes 6291456 | tf_op jit(solution)/shard_map/advect/pallas_call | solution.py:16
  30.4 38.1 %all_to_all.10 = bf16[64,16,512]{2,1,0:T(8,128)(2,1)S(1)} all-to-all(bf16[64,16,512]{2,1,0:T(8,128)(2,1)S(1)} %bitcast.6), channel_id=1, replica_groups=mesh['face'=16,'blk'=64] {'blk'}, dimensions={0} | all-to-all | bytes 2097152 | tf_op jit(solution)/shard_map/all_to_all | solution.py:269
  68.5 3.2 %net.1 = (bf16[1024,256]{1,0:T(8,128)(2,1)S(1)}, f32[32,32,128]{2,1,0:T(8,128)}) custom-call(bf16[1024,512]{1,0:T(8,128)(2,1)S(1)} %bitcast.7, bf16[1,512,512]{2,1,0:T(8,128)(2,1)S(1)} %copy-done.5, bf16[1,4,512,512]{3,2,1,0:T(8,128)(2,1)S(1)} %copy-done.4, bf16[1,512,256]{2,1,0:T(8,128)(2,1)S(1)} %copy-done.6, f32[32,32,128]{2,1,0:T(8,128)S(1)} %get-tuple-element.21.advected), custom_call_target="tpu_custom_call" | custom-call | flops 2952790016 | bytes 5242880 | tf_op jit(solution)/shard_map/net/pallas_call | solution.py:16
  71.7 26.4 %all_to_all.11 = bf16[64,16,256]{2,1,0:T(8,128)(2,1)S(1)} all-to-all(bf16[64,16,256]{2,1,0:T(8,128)(2,1)S(1)} %bitcast.8), channel_id=1, replica_groups=mesh['face'=16,'blk'=64] {'blk'}, dimensions={0} | all-to-all | bytes 1048576 | tf_op jit(solution)/shard_map/all_to_all | solution.py:282
  98.1 1.7 %unpack.1 = bf16[1024,256]{1,0:T(8,128)(2,1)} custom-call(s32[32,32]{1,0:T(8,128)S(1)} %get-tuple-element.17.target, bf16[1024,256]{1,0:T(8,128)(2,1)S(1)} %bitcast.9), custom_call_target="tpu_custom_call" | custom-call | flops 536870912 | bytes 1048576 | tf_op jit(solution)/shard_map/unpack/pallas_call | solution.py:16
  (5 shorter events, 0.0 us)
Async XLA Ops:
  0.6 28.5 %copy-start.2 = (bf16[32,32,128]{2,1,0:T(8,128)(2,1)S(1)}, bf16[32,32,128]{2,1,0:T(8,128)(2,1)}, u32[]{:S(2)}) copy-start(bf16[32,32,128]{2,1,0:T(8,128)(2,1)} %wind_y.3) | copy-start | bytes 786436
  0.6 28.5 %copy-start.1 = (bf16[32,32,128]{2,1,0:T(8,128)(2,1)S(1)}, bf16[32,32,128]{2,1,0:T(8,128)(2,1)}, u32[]{:S(2)}) copy-start(bf16[32,32,128]{2,1,0:T(8,128)(2,1)} %wind_x.3) | copy-start | bytes 786436
  0.7 28.5 %copy-start = (f32[32,32,128]{2,1,0:T(8,128)S(1)}, f32[32,32,128]{2,1,0:T(8,128)}, u32[]{:S(2)}) copy-start(f32[32,32,128]{2,1,0:T(8,128)} %tracer.3) | copy-start | bytes 1572868
  0.7 28.5 %copy-start.3 = (f32[32,32]{1,0:T(8,128)S(1)}, f32[32,32]{1,0:T(8,128)}, u32[]{:S(2)}) copy-start(f32[32,32]{1,0:T(8,128)} %area.1) | copy-start | bytes 12292
  1.9 27.1 %collective-permute-start = (f32[2,32,128]{2,1,0:T(8,128)S(1)}, f32[2,32,128]{2,1,0:T(8,128)S(1)}, u32[]{:S(2)}, u32[]{:S(2)}) collective-permute-start(f32[2,32,128]{2,1,0:T(8,128)S(1)} %get-tuple-element.13), channel_id=1, source_target_pairs={{0,1},{1,2},{2,3},{3,4},{4,5},{5,6},{6,7},{7,8},{8,9},{9,10},{10,1... | collective-permute-start | bytes 98312 | tf_op jit(solution)/shard_map/ppermute | solution.py:247
  5.5 23.5 %collective-permute-start.1 = (f32[2,32,128]{2,1,0:T(8,128)S(1)}, f32[2,32,128]{2,1,0:T(8,128)S(1)}, u32[]{:S(2)}, u32[]{:S(2)}) collective-permute-start(f32[2,32,128]{2,1,0:T(8,128)S(1)} %get-tuple-element.14), channel_id=1, source_target_pairs={{1,0},{2,1},{3,2},{4,3},{5,4},{6,5},{7,6},{8,7},{9,8},{10,9},{11,1... | collective-permute-start | bytes 98312 | tf_op jit(solution)/shard_map/ppermute | solution.py:248
  24.9 4.2 %collective-permute-start.2 = (f32[2,32,128]{2,1,0:T(8,128)S(1)}, f32[2,32,128]{2,1,0:T(8,128)S(1)}, u32[]{:S(2)}, u32[]{:S(2)}) collective-permute-start(f32[2,32,128]{2,1,0:T(8,128)S(1)} %get-tuple-element.15), channel_id=1, source_target_pairs={{0,64},{64,128},{128,192},{192,256},{256,320},{320,384},{384,448},... | collective-permute-start | bytes 98312 | tf_op jit(solution)/shard_map/ppermute | solution.py:244
  24.9 4.2 %collective-permute-start.3 = (f32[2,32,128]{2,1,0:T(8,128)S(1)}, f32[2,32,128]{2,1,0:T(8,128)S(1)}, u32[]{:S(2)}, u32[]{:S(2)}) collective-permute-start(f32[2,32,128]{2,1,0:T(8,128)S(1)} %get-tuple-element.16), channel_id=1, source_target_pairs={{64,0},{128,64},{192,128},{256,192},{320,256},{384,320},{448,384},... | collective-permute-start | bytes 98312 | tf_op jit(solution)/shard_map/ppermute | solution.py:245
  29.1 39.4 %copy-start.4 = (bf16[1,4,512,512]{3,2,1,0:T(8,128)(2,1)S(1)}, bf16[1,4,512,512]{3,2,1,0:T(8,128)(2,1)}, u32[]{:S(2)}) copy-start(bf16[1,4,512,512]{3,2,1,0:T(8,128)(2,1)} %w_hidden.1) | copy-start | bytes 6291460
  29.1 39.4 %copy-start.5 = (bf16[1,512,512]{2,1,0:T(8,128)(2,1)S(1)}, bf16[1,512,512]{2,1,0:T(8,128)(2,1)}, u32[]{:S(2)}) copy-start(bf16[1,512,512]{2,1,0:T(8,128)(2,1)} %w_in.1) | copy-start | bytes 1572868
  29.2 39.3 %copy-start.6 = (bf16[1,512,256]{2,1,0:T(8,128)(2,1)S(1)}, bf16[1,512,256]{2,1,0:T(8,128)(2,1)}, u32[]{:S(2)}) copy-start(bf16[1,512,256]{2,1,0:T(8,128)(2,1)} %w_out.1) | copy-start | bytes 786436

commit v4 on v3

--- a/solution.py
+++ b/solution.py
@@ -118,10 +118,10 @@
     wind_x,
     wind_y,
     area,
+    west,
+    east,
     south,
     north,
-    west,
-    east,
     to_slots,
     packed_forcing,
     advected,
@@ -260,7 +260,7 @@
     advected, features = call(
         advect_kernel,
         [shaped(tracer.shape, f32), shaped((columns, width), bf16)],
-        [tracer, wind_x, wind_y, cell_area, south, north, west, east, to_slots, packed_forcing],
+        [tracer, wind_x, wind_y, cell_area, west, east, south, north, to_slots, packed_forcing],
         "advect",
         flops=2 * columns * columns * levels,
         touched=6 << 20,

time: 100 us -> 98.9 us (0.989)
  the two profiles are of different devices: /device:TPU:14 before, /device:TPU:6 now
where the time goes in v4:
time: 98.9 us; the launch traced here: 98.6 us
  blocking collectives  63.3 us (64%)
  starting transfers between devices  24.7 us (25%)
  Pallas kernels  9.76 us (10%)
    all_to_all x1, blocking collectives, local(): lax.all_to_all(features.reshape(groups, slots_per, width), 'blk', split_a...  37.7 us
    all_to_all x1, blocking collectives, local(): lax.all_to_all(result.reshape(groups, slots_per, width_out), 'blk', split...  25.6 us
    ppermute x1, starting transfers between devices, local(): north = lax.ppermute(first_y, 'blk', backward)  19.3 us
    pallas_call x5, Pallas kernels, call(): pl.pallas_call(kernel, out_shape=outs, in_specs=specs or [VMEM] * len(ope...  9.76 us
    ppermute x1, starting transfers between devices, local(): south = lax.ppermute(last_y, 'blk', forward)  3.59 us
  transfers between devices with their start and end apart: 4, of which 0 were waited for; matrix products, arithmetic and copies ran while one was open for 0% of the time, Pallas kernels for 2%

profile of v4, /device:TPU:6, one launch (start us, length us, event | category | flops | bytes accessed | tf_op | source)
XLA Modules:
  0.0 98.6 jit_solution(6937818857584518980)
XLA Ops:
  0.6 0.0 copy-start.2
  0.6 0.0 copy-start.1
  0.7 0.0 copy-start
  0.7 0.0 copy-start.3
  0.7 1.3 %edges.1 = (f32[2,32,128]{2,1,0:T(8,128)S(1)}, f32[2,32,128]{2,1,0:T(8,128)S(1)}, f32[2,32,128]{2,1,0:T(8,128)S(1)}, f32[2,32,128]{2,1,0:T(8,128)S(1)}, s32[32,32]{1,0:T(8,128)S(1)}) custom-call(f32[32,32,128]{2,1,0:T(8,128)} %tracer.3, bf16[32,32,128]{2,1,0:T(8,128)(2,1)} %wind_x.3, bf16[32,32,128]{2,1,0:T(8,128)(2,1)} %wind_y.3, s32[32,32]{1,0:T(8,128)} %target.1), custom_call_target="tpu_custom_call" | custom-call | bytes 524288 | tf_op jit(solution)/shard_map/edges/pallas_call | solution.py:16
  1.9 0.0 collective-permute-start
  2.0 1.7 %collective-permute-start.1 = (f32[2,32,128]{2,1,0:T(8,128)S(1)}, f32[2,32,128]{2,1,0:T(8,128)S(1)}, u32[]{:S(2)}, u32[]{:S(2)}) collective-permute-start(f32[2,32,128]{2,1,0:T(8,128)S(1)} %get-tuple-element.14), channel_id=1, source_target_pairs={{64,0},{128,64},{192,128},{256,192},{320,256},{384,320},{448,384},... | collective-permute-start | bytes 98312 | tf_op jit(solution)/shard_map/ppermute | solution.py:245
  3.7 3.6 %collective-permute-start.2 = (f32[2,32,128]{2,1,0:T(8,128)S(1)}, f32[2,32,128]{2,1,0:T(8,128)S(1)}, u32[]{:S(2)}, u32[]{:S(2)}) collective-permute-start(f32[2,32,128]{2,1,0:T(8,128)S(1)} %get-tuple-element.15), channel_id=1, source_target_pairs={{0,1},{1,2},{2,3},{3,4},{4,5},{5,6},{6,7},{7,8},{8,9},{9,10},{10,1... | collective-permute-start | bytes 98312 | tf_op jit(solution)/shard_map/ppermute | solution.py:247
  7.3 19.3 %collective-permute-start.3 = (f32[2,32,128]{2,1,0:T(8,128)S(1)}, f32[2,32,128]{2,1,0:T(8,128)S(1)}, u32[]{:S(2)}, u32[]{:S(2)}) collective-permute-start(f32[2,32,128]{2,1,0:T(8,128)S(1)} %get-tuple-element.16), channel_id=1, source_target_pairs={{1,0},{2,1},{3,2},{4,3},{5,4},{6,5},{7,6},{8,7},{9,8},{10,9},{11,1... | collective-permute-start | bytes 98312 | tf_op jit(solution)/shard_map/ppermute | solution.py:248
  26.6 2.4 %select.1 = (bf16[1024,1024]{1,0:T(8,128)(2,1)S(1)}, bf16[1024,384]{1,0:T(8,128)(2,1)S(1)}) custom-call(s32[32,32]{1,0:T(8,128)S(1)} %get-tuple-element.17.target, bf16[1024,384]{1,0:T(8,128)(2,1)} %bitcast.10), custom_call_target="tpu_custom_call" | custom-call | flops 805306368 | bytes 4194304 | tf_op jit(solution)/shard_map/select/pallas_call | solution.py:16
  29.0 0.0 collective-permute-done.west
  29.1 0.0 collective-permute-done.1.east
  29.1 0.0 collective-permute-done.2.south
  29.1 0.0 collective-permute-done.3.north
  29.1 0.0 copy-done.2
  29.1 0.0 copy-start.4
  29.1 0.0 copy-start.5
  29.1 0.0 copy-start.6
  29.2 1.3 %advect.1 = (f32[32,32,128]{2,1,0:T(8,128)S(1)}, bf16[1024,512]{1,0:T(8,128)(2,1)S(1)}) custom-call(f32[32,32,128]{2,1,0:T(8,128)S(1)} %copy-done, bf16[32,32,128]{2,1,0:T(8,128)(2,1)S(1)} %copy-done.1, bf16[32,32,128]{2,1,0:T(8,128)(2,1)S(1)} %copy-done.2, f32[32,32]{1,0:T(8,128)S(1)} %copy-done.3, f32[2,32,128]{2,1,0:T(8,128)S(1)} %collective-permute-done.west, ...), custom_call_target="tpu_custom_call" | custom-call | flops 268435456 | bytes 6291456 | tf_op jit(solution)/shard_map/advect/pallas_call | solution.py:16
  30.4 37.7 %all_to_all.10 = bf16[64,16,512]{2,1,0:T(8,128)(2,1)S(1)} all-to-all(bf16[64,16,512]{2,1,0:T(8,128)(2,1)S(1)} %bitcast.6), channel_id=1, replica_groups=mesh['face'=16,'blk'=64] {'blk'}, dimensions={0} | all-to-all | bytes 2097152 | tf_op jit(solution)/shard_map/all_to_all | solution.py:269
  68.1 0.0 copy-done.5
  68.1 3.2 %net.1 = (bf16[1024,256]{1,0:T(8,128)(2,1)S(1)}, f32[32,32,128]{2,1,0:T(8,128)}) custom-call(bf16[1024,512]{1,0:T(8,128)(2,1)S(1)} %bitcast.7, bf16[1,512,512]{2,1,0:T(8,128)(2,1)S(1)} %copy-done.5, bf16[1,4,512,512]{3,2,1,0:T(8,128)(2,1)S(1)} %copy-done.4, bf16[1,512,256]{2,1,0:T(8,128)(2,1)S(1)} %copy-done.6, f32[32,32,128]{2,1,0:T(8,128)S(1)} %get-tuple-element.21.advected), custom_call_target="tpu_custom_call" | custom-call | flops 2952790016 | bytes 5242880 | tf_op jit(solution)/shard_map/net/pallas_call | solution.py:16
  71.3 25.6 %all_to_all.11 = bf16[64,16,256]{2,1,0:T(8,128)(2,1)S(1)} all-to-all(bf16[64,16,256]{2,1,0:T(8,128)(2,1)S(1)} %bitcast.8), channel_id=1, replica_groups=mesh['face'=16,'blk'=64] {'blk'}, dimensions={0} | all-to-all | bytes 1048576 | tf_op jit(solution)/shard_map/all_to_all | solution.py:282
  96.9 1.7 %unpack.1 = bf16[1024,256]{1,0:T(8,128)(2,1)} custom-call(s32[32,32]{1,0:T(8,128)S(1)} %get-tuple-element.17.target, bf16[1024,256]{1,0:T(8,128)(2,1)S(1)} %bitcast.9), custom_call_target="tpu_custom_call" | custom-call | flops 536870912 | bytes 1048576 | tf_op jit(solution)/shard_map/unpack/pallas_call | solution.py:16
  (5 shorter events, 0.0 us)
Async XLA Ops:
  0.6 28.5 %copy-start.2 = (bf16[32,32,128]{2,1,0:T(8,128)(2,1)S(1)}, bf16[32,32,128]{2,1,0:T(8,128)(2,1)}, u32[]{:S(2)}) copy-start(bf16[32,32,128]{2,1,0:T(8,128)(2,1)} %wind_y.3) | copy-start | bytes 786436
  0.6 28.5 %copy-start.1 = (bf16[32,32,128]{2,1,0:T(8,128)(2,1)S(1)}, bf16[32,32,128]{2,1,0:T(8,128)(2,1)}, u32[]{:S(2)}) copy-start(bf16[32,32,128]{2,1,0:T(8,128)(2,1)} %wind_x.3) | copy-start | bytes 786436
  0.7 28.5 %copy-start = (f32[32,32,128]{2,1,0:T(8,128)S(1)}, f32[32,32,128]{2,1,0:T(8,128)}, u32[]{:S(2)}) copy-start(f32[32,32,128]{2,1,0:T(8,128)} %tracer.3) | copy-start | bytes 1572868
  0.7 28.5 %copy-start.3 = (f32[32,32]{1,0:T(8,128)S(1)}, f32[32,32]{1,0:T(8,128)}, u32[]{:S(2)}) copy-start(f32[32,32]{1,0:T(8,128)} %area.1) | copy-start | bytes 12292
  1.9 27.1 %collective-permute-start = (f32[2,32,128]{2,1,0:T(8,128)S(1)}, f32[2,32,128]{2,1,0:T(8,128)S(1)}, u32[]{:S(2)}, u32[]{:S(2)}) collective-permute-start(f32[2,32,128]{2,1,0:T(8,128)S(1)} %get-tuple-element.13), channel_id=1, source_target_pairs={{0,64},{64,128},{128,192},{192,256},{256,320},{320,384},{384,448},... | collective-permute-start | bytes 98312 | tf_op jit(solution)/shard_map/ppermute | solution.py:244
  2.0 27.1 %collective-permute-start.1 = (f32[2,32,128]{2,1,0:T(8,128)S(1)}, f32[2,32,128]{2,1,0:T(8,128)S(1)}, u32[]{:S(2)}, u32[]{:S(2)}) collective-permute-start(f32[2,32,128]{2,1,0:T(8,128)S(1)} %get-tuple-element.14), channel_id=1, source_target_pairs={{64,0},{128,64},{192,128},{256,192},{320,256},{384,320},{448,384},... | collective-permute-start | bytes 98312 | tf_op jit(solution)/shard_map/ppermute | solution.py:245
  3.7 25.4 %collective-permute-start.2 = (f32[2,32,128]{2,1,0:T(8,128)S(1)}, f32[2,32,128]{2,1,0:T(8,128)S(1)}, u32[]{:S(2)}, u32[]{:S(2)}) collective-permute-start(f32[2,32,128]{2,1,0:T(8,128)S(1)} %get-tuple-element.15), channel_id=1, source_target_pairs={{0,1},{1,2},{2,3},{3,4},{4,5},{5,6},{6,7},{7,8},{8,9},{9,10},{10,1... | collective-permute-start | bytes 98312 | tf_op jit(solution)/shard_map/ppermute | solution.py:247
  7.3 21.8 %collective-permute-start.3 = (f32[2,32,128]{2,1,0:T(8,128)S(1)}, f32[2,32,128]{2,1,0:T(8,128)S(1)}, u32[]{:S(2)}, u32[]{:S(2)}) collective-permute-start(f32[2,32,128]{2,1,0:T(8,128)S(1)} %get-tuple-element.16), channel_id=1, source_target_pairs={{1,0},{2,1},{3,2},{4,3},{5,4},{6,5},{7,6},{8,7},{9,8},{10,9},{11,1... | collective-permute-start | bytes 98312 | tf_op jit(solution)/shard_map/ppermute | solution.py:248
  29.1 39.0 %copy-start.4 = (bf16[1,4,512,512]{3,2,1,0:T(8,128)(2,1)S(1)}, bf16[1,4,512,512]{3,2,1,0:T(8,128)(2,1)}, u32[]{:S(2)}) copy-start(bf16[1,4,512,512]{3,2,1,0:T(8,128)(2,1)} %w_hidden.1) | copy-start | bytes 6291460
  29.1 39.0 %copy-start.5 = (bf16[1,512,512]{2,1,0:T(8,128)(2,1)S(1)}, bf16[1,512,512]{2,1,0:T(8,128)(2,1)}, u32[]{:S(2)}) copy-start(bf16[1,512,512]{2,1,0:T(8,128)(2,1)} %w_in.1) | copy-start | bytes 1572868
  29.1 39.0 %copy-start.6 = (bf16[1,512,256]{2,1,0:T(8,128)(2,1)S(1)}, bf16[1,512,256]{2,1,0:T(8,128)(2,1)}, u32[]{:S(2)}) copy-start(bf16[1,512,256]{2,1,0:T(8,128)(2,1)} %w_out.1) | copy-start | bytes 786436

commit v5 on v4

--- a/solution.py
+++ b/solution.py
@@ -93,9 +93,7 @@
     return jnp.sum(own, axis=0, keepdims=True).astype(jnp.int32)
 
 
-def select_kernel(target, forcing, to_slots, packed, rows, arrived):
-    copy = pltpu.make_async_copy(forcing, rows, arrived)
-    copy.start()
+def fill_slots(target, to_slots):
     slots, columns = to_slots.shape
     step = 128
     row = row_of(target[...], columns)
@@ -107,10 +105,18 @@
         return 0
 
     lax.fori_loop(0, slots // step, body, 0)
-    copy.wait()
-    packed[...] = jnp.dot(
-        to_slots[...], rows[...], preferred_element_type=jnp.float32
-    ).astype(jnp.bfloat16)
+
+
+def select_kernel(target, forcing, to_slots, packed, rows, arrived):
+    @pl.when(lax.axis_index("face") % 2 == 1)
+    def _():
+        copy = pltpu.make_async_copy(forcing, rows, arrived)
+        copy.start()
+        fill_slots(target, to_slots)
+        copy.wait()
+        packed[...] = jnp.dot(
+            to_slots[...], rows[...], preferred_element_type=jnp.float32
+        ).astype(jnp.bfloat16)
 
 
 def advect_kernel(
@@ -124,11 +130,23 @@
     north,
     to_slots,
     packed_forcing,
+    target,
+    forcing,
     advected,
     features,
     rounded,
+    own_slots,
+    rows,
+    arrived,
 ):
     cells_x, cells_y, levels = tracer.shape
+    second = lax.axis_index("face") % 2 == 0
+    copy = pltpu.make_async_copy(forcing, rows, arrived)
+
+    @pl.when(second)
+    def _():
+        copy.start()
+
     inverse = jnp.transpose(1.0 / area[...])
     place = lax.broadcasted_iota(jnp.int32, (cells_y, levels), 0)
     west_speed = west[1]
@@ -154,10 +172,30 @@
         advected[i] = moved
         rounded[i * cells_y : (i + 1) * cells_y, :] = moved.astype(jnp.bfloat16)
         flux_before = flux_x
-    features[:, levels:] = packed_forcing[...]
-    features[:, :levels] = jnp.dot(
-        to_slots[...], rounded[...], preferred_element_type=jnp.float32
-    ).astype(jnp.bfloat16)
+
+    def put(part, values):
+        features[:, part] = values.astype(jnp.bfloat16)
+
+    @pl.when(jnp.logical_not(second))
+    def _():
+        features[:, levels:] = packed_forcing[...]
+        put(
+            slice(0, levels),
+            jnp.dot(to_slots[...], rounded[...], preferred_element_type=jnp.float32),
+        )
+
+    @pl.when(second)
+    def _():
+        fill_slots(target, own_slots)
+        put(
+            slice(0, levels),
+            jnp.dot(own_slots[...], rounded[...], preferred_element_type=jnp.float32),
+        )
+        copy.wait()
+        put(
+            slice(levels, features.shape[1]),
+            jnp.dot(own_slots[...], rows[...], preferred_element_type=jnp.float32),
+        )
 
 
 def net_kernel(
@@ -260,11 +298,30 @@
     advected, features = call(
         advect_kernel,
         [shaped(tracer.shape, f32), shaped((columns, width), bf16)],
-        [tracer, wind_x, wind_y, cell_area, west, east, south, north, to_slots, packed_forcing],
+        [
+            tracer,
+            wind_x,
+            wind_y,
+            cell_area,
+            west,
+            east,
+            south,
+            north,
+            to_slots,
+            packed_forcing,
+            target,
+            in_hbm(forcing.reshape(columns, forcing.shape[2])),
+        ],
         "advect",
         flops=2 * columns * columns * levels,
         touched=6 << 20,
-        scratch=[pltpu.VMEM((columns, levels), bf16)],
+        scratch=[
+            pltpu.VMEM((columns, levels), bf16),
+            pltpu.VMEM((columns, columns), bf16),
+            pltpu.VMEM((columns, forcing.shape[2]), bf16),
+            pltpu.SemaphoreType.DMA,
+        ],
+        specs=[VMEM] * 11 + [HBM],
     )
     received = lax.all_to_all(
         features.reshape(groups, slots_per, width), "blk", split_axis=0, concat_axis=0, tiled=True

time: 98.9 us -> 97.5 us (0.986)
  blocking collectives: 63.3 us -> 61 us
  waiting for transfers between devices: 0.01 us -> 1.6 us
    all_to_all x1, blocking collectives: 25.6 us -> 23.9 us  [local(): lax.all_to_all(result.reshape(groups, slots_per, width_out), 'blk', split...]
    ppermute x1, waiting for transfers between devices: 0.01 us -> 1.59 us  [local(): north = lax.ppermute(first_y, 'blk', backward)]
  transfers between devices with their start and end apart: 4 -> 4, of which waited for: 0 -> 1; matrix products, arithmetic and copies ran while one was open for 0% -> 0% of each run, Pallas kernels for 2% -> 0%
where the time goes in v5:
time: 97.5 us; the launch traced here: 97.2 us
  blocking collectives  61 us (63%)
  starting transfers between devices  24.7 us (25%)
  Pallas kernels  9.17 us (9%)
  waiting for transfers between devices  1.6 us (2%)
    all_to_all x1, blocking collectives, local(): lax.all_to_all(features.reshape(groups, slots_per, width), 'blk', split_a...  37 us
    all_to_all x1, blocking collectives, local(): lax.all_to_all(result.reshape(groups, slots_per, width_out), 'blk', split...  23.9 us
    ppermute x1, starting transfers between devices, local(): north = lax.ppermute(first_y, 'blk', backward)  19.3 us
    pallas_call x5, Pallas kernels, call(): pl.pallas_call(kernel, out_shape=outs, in_specs=specs or [VMEM] * len(ope...  9.17 us
    ppermute x1, starting transfers between devices, local(): south = lax.ppermute(last_y, 'blk', forward)  3.59 us
  transfers between devices with their start and end apart: 4, of which 1 were waited for; matrix products, arithmetic and copies ran while one was open for 0% of the time, Pallas kernels for 0%

profile of v5, /device:TPU:6, one launch (start us, length us, event | category | flops | bytes accessed | tf_op | source)
XLA Modules:
  0.0 97.2 jit_solution(17727975473416163018)
XLA Ops:
  0.6 0.0 copy-start.2
  0.6 0.0 copy-start.1
  0.7 0.0 copy-start
  0.7 0.0 copy-start.3
  0.7 1.3 %edges.1 = (f32[2,32,128]{2,1,0:T(8,128)S(1)}, f32[2,32,128]{2,1,0:T(8,128)S(1)}, f32[2,32,128]{2,1,0:T(8,128)S(1)}, f32[2,32,128]{2,1,0:T(8,128)S(1)}, s32[32,32]{1,0:T(8,128)S(1)}) custom-call(f32[32,32,128]{2,1,0:T(8,128)} %tracer.3, bf16[32,32,128]{2,1,0:T(8,128)(2,1)} %wind_x.3, bf16[32,32,128]{2,1,0:T(8,128)(2,1)} %wind_y.3, s32[32,32]{1,0:T(8,128)} %target.1), custom_call_target="tpu_custom_call" | custom-call | bytes 524288 | tf_op jit(solution)/shard_map/edges/pallas_call | solution.py:16
  1.9 0.0 collective-permute-start
  2.0 1.7 %collective-permute-start.1 = (f32[2,32,128]{2,1,0:T(8,128)S(1)}, f32[2,32,128]{2,1,0:T(8,128)S(1)}, u32[]{:S(2)}, u32[]{:S(2)}) collective-permute-start(f32[2,32,128]{2,1,0:T(8,128)S(1)} %get-tuple-element.14), channel_id=1, source_target_pairs={{64,0},{128,64},{192,128},{256,192},{320,256},{384,320},{448,384},... | collective-permute-start | bytes 98312 | tf_op jit(solution)/shard_map/ppermute | solution.py:283
  3.7 3.6 %collective-permute-start.2 = (f32[2,32,128]{2,1,0:T(8,128)S(1)}, f32[2,32,128]{2,1,0:T(8,128)S(1)}, u32[]{:S(2)}, u32[]{:S(2)}) collective-permute-start(f32[2,32,128]{2,1,0:T(8,128)S(1)} %get-tuple-element.15), channel_id=1, source_target_pairs={{0,1},{1,2},{2,3},{3,4},{4,5},{5,6},{6,7},{7,8},{8,9},{9,10},{10,1... | collective-permute-start | bytes 98312 | tf_op jit(solution)/shard_map/ppermute | solution.py:285
  7.3 19.3 %collective-permute-start.3 = (f32[2,32,128]{2,1,0:T(8,128)S(1)}, f32[2,32,128]{2,1,0:T(8,128)S(1)}, u32[]{:S(2)}, u32[]{:S(2)}) collective-permute-start(f32[2,32,128]{2,1,0:T(8,128)S(1)} %get-tuple-element.16), channel_id=1, source_target_pairs={{1,0},{2,1},{3,2},{4,3},{5,4},{6,5},{7,6},{8,7},{9,8},{10,9},{11,1... | collective-permute-start | bytes 98312 | tf_op jit(solution)/shard_map/ppermute | solution.py:286
  26.7 0.0 collective-permute-done.west
  26.7 0.0 collective-permute-done.1.east
  26.7 0.0 collective-permute-done.2.south
  26.7 1.6 %collective-permute-done.3.north = f32[2,32,128]{2,1,0:T(8,128)S(1)} collective-permute-done((f32[2,32,128]{2,1,0:T(8,128)S(1)}, f32[2,32,128]{2,1,0:T(8,128)S(1)}, u32[]{:S(2)}, u32[]{:S(2)}) %collective-permute-start.3) | collective-permute-done | bytes 32800 | tf_op jit(solution)/shard_map/ppermute | solution.py:286
  28.3 0.0 copy-done.2
  28.3 0.0 copy-done.1
  28.3 0.0 copy-done.3
  28.3 0.0 copy-start.5
  28.3 0.0 copy-start.6
  28.3 3.0 %advect.1 = (f32[32,32,128]{2,1,0:T(8,128)S(1)}, bf16[1024,512]{1,0:T(8,128)(2,1)S(1)}) custom-call(f32[32,32,128]{2,1,0:T(8,128)S(1)} %copy-done, bf16[32,32,128]{2,1,0:T(8,128)(2,1)S(1)} %copy-done.1, bf16[32,32,128]{2,1,0:T(8,128)(2,1)S(1)} %copy-done.2, f32[32,32]{1,0:T(8,128)S(1)} %copy-done.3, f32[2,32,128]{2,1,0:T(8,128)S(1)} %collective-permute-done.west, ...), custom_call_target="tpu_custom_call" | custom-call | flops 268435456 | bytes 6291456 | tf_op jit(solution)/shard_map/advect/pallas_call | solution.py:16
  31.4 0.0 copy-start.4
  31.4 37.0 %all_to_all.10 = bf16[64,16,512]{2,1,0:T(8,128)(2,1)S(1)} all-to-all(bf16[64,16,512]{2,1,0:T(8,128)(2,1)S(1)} %bitcast.6), channel_id=1, replica_groups=mesh['face'=16,'blk'=64] {'blk'}, dimensions={0} | all-to-all | bytes 2097152 | tf_op jit(solution)/shard_map/all_to_all | solution.py:326
  68.4 3.2 %net.1 = (bf16[1024,256]{1,0:T(8,128)(2,1)S(1)}, f32[32,32,128]{2,1,0:T(8,128)}) custom-call(bf16[1024,512]{1,0:T(8,128)(2,1)S(1)} %bitcast.7, bf16[1,512,512]{2,1,0:T(8,128)(2,1)S(1)} %copy-done.5, bf16[1,4,512,512]{3,2,1,0:T(8,128)(2,1)S(1)} %copy-done.4, bf16[1,512,256]{2,1,0:T(8,128)(2,1)S(1)} %copy-done.6, f32[32,32,128]{2,1,0:T(8,128)S(1)} %get-tuple-element.21.advected), custom_call_target="tpu_custom_call" | custom-call | flops 2952790016 | bytes 5242880 | tf_op jit(solution)/shard_map/net/pallas_call | solution.py:16
  71.6 23.9 %all_to_all.11 = bf16[64,16,256]{2,1,0:T(8,128)(2,1)S(1)} all-to-all(bf16[64,16,256]{2,1,0:T(8,128)(2,1)S(1)} %bitcast.8), channel_id=1, replica_groups=mesh['face'=16,'blk'=64] {'blk'}, dimensions={0} | all-to-all | bytes 1048576 | tf_op jit(solution)/shard_map/all_to_all | solution.py:339
  95.5 1.7 %unpack.1 = bf16[1024,256]{1,0:T(8,128)(2,1)} custom-call(s32[32,32]{1,0:T(8,128)S(1)} %get-tuple-element.17.target, bf16[1024,256]{1,0:T(8,128)(2,1)S(1)} %bitcast.9), custom_call_target="tpu_custom_call" | custom-call | flops 536870912 | bytes 1048576 | tf_op jit(solution)/shard_map/unpack/pallas_call | solution.py:16
  (5 shorter events, 0.0 us)
Async XLA Ops:
  0.6 27.7 %copy-start.2 = (bf16[32,32,128]{2,1,0:T(8,128)(2,1)S(1)}, bf16[32,32,128]{2,1,0:T(8,128)(2,1)}, u32[]{:S(2)}) copy-start(bf16[32,32,128]{2,1,0:T(8,128)(2,1)} %wind_y.3) | copy-start | bytes 786436
  0.6 27.7 %copy-start.1 = (bf16[32,32,128]{2,1,0:T(8,128)(2,1)S(1)}, bf16[32,32,128]{2,1,0:T(8,128)(2,1)}, u32[]{:S(2)}) copy-start(bf16[32,32,128]{2,1,0:T(8,128)(2,1)} %wind_x.3) | copy-start | bytes 786436
  0.7 27.7 %copy-start = (f32[32,32,128]{2,1,0:T(8,128)S(1)}, f32[32,32,128]{2,1,0:T(8,128)}, u32[]{:S(2)}) copy-start(f32[32,32,128]{2,1,0:T(8,128)} %tracer.3) | copy-start | bytes 1572868
  0.7 27.6 %copy-start.3 = (f32[32,32]{1,0:T(8,128)S(1)}, f32[32,32]{1,0:T(8,128)}, u32[]{:S(2)}) copy-start(f32[32,32]{1,0:T(8,128)} %area.1) | copy-start | bytes 12292
  1.9 24.7 %collective-permute-start = (f32[2,32,128]{2,1,0:T(8,128)S(1)}, f32[2,32,128]{2,1,0:T(8,128)S(1)}, u32[]{:S(2)}, u32[]{:S(2)}) collective-permute-start(f32[2,32,128]{2,1,0:T(8,128)S(1)} %get-tuple-element.13), channel_id=1, source_target_pairs={{0,64},{64,128},{128,192},{192,256},{256,320},{320,384},{384,448},... | collective-permute-start | bytes 98312 | tf_op jit(solution)/shard_map/ppermute | solution.py:282
  2.0 24.7 %collective-permute-start.1 = (f32[2,32,128]{2,1,0:T(8,128)S(1)}, f32[2,32,128]{2,1,0:T(8,128)S(1)}, u32[]{:S(2)}, u32[]{:S(2)}) collective-permute-start(f32[2,32,128]{2,1,0:T(8,128)S(1)} %get-tuple-element.14), channel_id=1, source_target_pairs={{64,0},{128,64},{192,128},{256,192},{320,256},{384,320},{448,384},... | collective-permute-start | bytes 98312 | tf_op jit(solution)/shard_map/ppermute | solution.py:283
  3.7 23.0 %collective-permute-start.2 = (f32[2,32,128]{2,1,0:T(8,128)S(1)}, f32[2,32,128]{2,1,0:T(8,128)S(1)}, u32[]{:S(2)}, u32[]{:S(2)}) collective-permute-start(f32[2,32,128]{2,1,0:T(8,128)S(1)} %get-tuple-element.15), channel_id=1, source_target_pairs={{0,1},{1,2},{2,3},{3,4},{4,5},{5,6},{6,7},{7,8},{8,9},{9,10},{10,1... | collective-permute-start | bytes 98312 | tf_op jit(solution)/shard_map/ppermute | solution.py:285
  7.3 21.0 %collective-permute-start.3 = (f32[2,32,128]{2,1,0:T(8,128)S(1)}, f32[2,32,128]{2,1,0:T(8,128)S(1)}, u32[]{:S(2)}, u32[]{:S(2)}) collective-permute-start(f32[2,32,128]{2,1,0:T(8,128)S(1)} %get-tuple-element.16), channel_id=1, source_target_pairs={{1,0},{2,1},{3,2},{4,3},{5,4},{6,5},{7,6},{8,7},{9,8},{10,9},{11,1... | collective-permute-start | bytes 98312 | tf_op jit(solution)/shard_map/ppermute | solution.py:286
  28.3 40.1 %copy-start.5 = (bf16[1,512,512]{2,1,0:T(8,128)(2,1)S(1)}, bf16[1,512,512]{2,1,0:T(8,128)(2,1)}, u32[]{:S(2)}) copy-start(bf16[1,512,512]{2,1,0:T(8,128)(2,1)} %w_in.1) | copy-start | bytes 1572868
  28.3 40.1 %copy-start.6 = (bf16[1,512,256]{2,1,0:T(8,128)(2,1)S(1)}, bf16[1,512,256]{2,1,0:T(8,128)(2,1)}, u32[]{:S(2)}) copy-start(bf16[1,512,256]{2,1,0:T(8,128)(2,1)} %w_out.1) | copy-start | bytes 786436
  31.4 37.1 %copy-start.4 = (bf16[1,4,512,512]{3,2,1,0:T(8,128)(2,1)S(1)}, bf16[1,4,512,512]{3,2,1,0:T(8,128)(2,1)}, u32[]{:S(2)}) copy-start(bf16[1,4,512,512]{3,2,1,0:T(8,128)(2,1)} %w_hidden.1) | copy-start | bytes 6291460

commit v6 on v5

--- a/solution.py
+++ b/solution.py
@@ -34,11 +34,13 @@
     wind_x,
     wind_y,
     target,
+    forcing,
     last_x,
     first_x,
     last_y,
     first_y,
     held_target,
+    held_forcing,
     low_rows,
     high_rows,
     speed_x,
@@ -57,6 +59,7 @@
                 (tracer.at[:, pl.ds(cells_y - 8, 8), :], high_rows),
                 (wind_y.at[:, pl.ds(cells_y - 16, 16), :], speed_y),
                 (target, held_target),
+                (forcing, held_forcing),
             )
         )
     ]
@@ -107,15 +110,23 @@
     lax.fori_loop(0, slots // step, body, 0)
 
 
-def select_kernel(target, forcing, to_slots, packed, rows, arrived):
+def fill_columns(target, to_columns, rows):
+    cells_y = target.shape[1]
+    turned = jnp.transpose(target[...].astype(jnp.float32)).astype(jnp.int32)
+    place = lax.broadcasted_iota(jnp.int32, (cells_y, to_columns.shape[1]), 1)
+    for start in range(rows.start, rows.stop, cells_y):
+        i = start // cells_y
+        to_columns[start : start + cells_y, :] = jnp.where(
+            turned[:, i : i + 1] == place, 1.0, 0.0
+        ).astype(jnp.bfloat16)
+
+
+def select_kernel(target, forcing, to_slots, packed):
     @pl.when(lax.axis_index("face") % 2 == 1)
     def _():
-        copy = pltpu.make_async_copy(forcing, rows, arrived)
-        copy.start()
         fill_slots(target, to_slots)
-        copy.wait()
         packed[...] = jnp.dot(
-            to_slots[...], rows[...], preferred_element_type=jnp.float32
+            to_slots[...], forcing[...], preferred_element_type=jnp.float32
         ).astype(jnp.bfloat16)
 
 
@@ -134,19 +145,12 @@
     forcing,
     advected,
     features,
+    to_columns,
     rounded,
     own_slots,
-    rows,
-    arrived,
 ):
     cells_x, cells_y, levels = tracer.shape
     second = lax.axis_index("face") % 2 == 0
-    copy = pltpu.make_async_copy(forcing, rows, arrived)
-
-    @pl.when(second)
-    def _():
-        copy.start()
-
     inverse = jnp.transpose(1.0 / area[...])
     place = lax.broadcasted_iota(jnp.int32, (cells_y, levels), 0)
     west_speed = west[1]
@@ -186,15 +190,15 @@
 
     @pl.when(second)
     def _():
+        fill_columns(target, to_columns, slice(0, to_columns.shape[0]))
         fill_slots(target, own_slots)
         put(
             slice(0, levels),
             jnp.dot(own_slots[...], rounded[...], preferred_element_type=jnp.float32),
         )
-        copy.wait()
         put(
             slice(levels, features.shape[1]),
-            jnp.dot(own_slots[...], rows[...], preferred_element_type=jnp.float32),
+            jnp.dot(own_slots[...], forcing[...], preferred_element_type=jnp.float32),
         )
 
 
@@ -223,21 +227,26 @@
     copy.wait()
 
 
-def unpack_kernel(target, returned, tendencies, to_columns):
-    cells_x, cells_y = target.shape
-    slots = returned.shape[0]
-    turned = jnp.transpose(target[...].astype(jnp.float32)).astype(jnp.int32)
-    place = lax.broadcasted_iota(jnp.int32, (cells_y, slots), 1)
-    per = 8
-    for first in range(0, cells_x, per):
-        for i in range(first, first + per):
-            to_columns[i * cells_y : (i + 1) * cells_y, :] = jnp.where(
-                turned[:, i : i + 1] == place, 1.0, 0.0
-            ).astype(jnp.bfloat16)
-        rows = slice(first * cells_y, (first + per) * cells_y)
+def unpack_kernel(target, to_columns, returned, tendencies, own_columns):
+    columns = tendencies.shape[0]
+    step = 256
+
+    def take(one_hot, rows):
         tendencies[rows, :] = jnp.dot(
-            to_columns[rows, :], returned[...], preferred_element_type=jnp.float32
+            one_hot[rows, :], returned[...], preferred_element_type=jnp.float32
         ).astype(jnp.bfloat16)
+
+    @pl.when(lax.axis_index("face") % 2 == 0)
+    def _():
+        for start in range(0, columns, step):
+            take(to_columns, slice(start, start + step))
+
+    @pl.when(lax.axis_index("face") % 2 == 1)
+    def _():
+        for start in range(0, columns, step):
+            rows = slice(start, start + step)
+            fill_columns(target, own_columns, rows)
+            take(own_columns, rows)
 
 
 def neighbours(axis):
@@ -257,7 +266,7 @@
     shaped = pltpu.VMEM
     result_of = jax.ShapeDtypeStruct
 
-    last_x, first_x, last_y, first_y, target = call(
+    last_x, first_x, last_y, first_y, target, forcing = call(
         edges_kernel,
         [
             shaped((2, cells_y, levels), f32),
@@ -265,8 +274,12 @@
             shaped((2, cells_x, levels), f32),
             shaped((2, cells_x, levels), f32),
             shaped(group_map.shape, group_map.dtype),
-        ],
-        [in_hbm(tracer), in_hbm(wind_x), in_hbm(wind_y), in_hbm(group_map)],
+            shaped((columns, forcing.shape[2]), bf16),
+        ],
+        [
+            in_hbm(array)
+            for array in (tracer, wind_x, wind_y, group_map, forcing.reshape(columns, -1))
+        ],
         "edges",
         touched=1 << 19,
         scratch=[
@@ -274,9 +287,9 @@
             pltpu.VMEM((cells_x, 8, levels), f32),
             pltpu.VMEM((1, cells_y, levels), bf16),
             pltpu.VMEM((cells_x, 16, levels), bf16),
-            pltpu.SemaphoreType.DMA((7,)),
-        ],
-        specs=[HBM] * 4,
+            pltpu.SemaphoreType.DMA((8,)),
+        ],
+        specs=[HBM] * 5,
     )
     forward, backward = neighbours("face")
     west = lax.ppermute(last_x, "face", forward)
@@ -287,17 +300,19 @@
 
     to_slots, packed_forcing = call(
         select_kernel,
-        [shaped((columns, columns), bf16), shaped((columns, forcing.shape[2]), bf16)],
-        [target, in_hbm(forcing.reshape(columns, forcing.shape[2]))],
+        [shaped((columns, columns), bf16), shaped(forcing.shape, bf16)],
+        [target, forcing],
         "select",
-        flops=2 * columns * columns * forcing.shape[2],
+        flops=2 * columns * forcing.size,
         touched=4 << 20,
-        scratch=[pltpu.VMEM((columns, forcing.shape[2]), bf16), pltpu.SemaphoreType.DMA],
-        specs=[VMEM, HBM],
-    )
-    advected, features = call(
+    )
+    advected, features, to_columns = call(
         advect_kernel,
-        [shaped(tracer.shape, f32), shaped((columns, width), bf16)],
+        [
+            shaped(tracer.shape, f32),
+            shaped((columns, width), bf16),
+            shaped((columns, columns), bf16),
+        ],
         [
             tracer,
             wind_x,
@@ -310,7 +325,7 @@
             to_slots,
             packed_forcing,
             target,
-            in_hbm(forcing.reshape(columns, forcing.shape[2])),
+            forcing,
         ],
         "advect",
         flops=2 * columns * columns * levels,
@@ -318,10 +333,7 @@
         scratch=[
             pltpu.VMEM((columns, levels), bf16),
             pltpu.VMEM((columns, columns), bf16),
-            pltpu.VMEM((columns, forcing.shape[2]), bf16),
-            pltpu.SemaphoreType.DMA,
-        ],
-        specs=[VMEM] * 11 + [HBM],
+        ],
     )
     received = lax.all_to_all(
         features.reshape(groups, slots_per, width), "blk", split_axis=0, concat_axis=0, tiled=True
@@ -342,7 +354,7 @@
     tendencies = call(
         unpack_kernel,
         result_of((columns, width_out), bf16),
-        [target, returned.reshape(columns, width_out)],
+        [target, to_columns, returned.reshape(columns, width_out)],
         "unpack",
         flops=2 * columns * columns * width_out,
         touched=1 << 20,

time: 97.5 us -> 96.7 us (level)
  blocking collectives: 61 us -> 59.9 us
where the time goes in v6:
time: 96.7 us; the launch traced here: 96.5 us
  blocking collectives  59.9 us (62%)
  starting transfers between devices  24.7 us (26%)
  Pallas kernels  9.48 us (10%)
  waiting for transfers between devices  1.61 us (2%)
    all_to_all x1, blocking collectives, local(): lax.all_to_all(features.reshape(groups, slots_per, width), 'blk', split_a...  36.2 us
    all_to_all x1, blocking collectives, local(): lax.all_to_all(result.reshape(groups, slots_per, width_out), 'blk', split...  23.7 us
    ppermute x1, starting transfers between devices, local(): north = lax.ppermute(first_y, 'blk', backward)  19.3 us
    pallas_call x5, Pallas kernels, call(): pl.pallas_call(kernel, out_shape=outs, in_specs=specs or [VMEM] * len(ope...  9.48 us
    ppermute x1, starting transfers between devices, local(): south = lax.ppermute(last_y, 'blk', forward)  3.59 us
  transfers between devices with their start and end apart: 4, of which 1 were waited for; matrix products, arithmetic and copies ran while one was open for 0% of the time, Pallas kernels for 0%

profile of v6, /device:TPU:6, one launch (start us, length us, event | category | flops | bytes accessed | tf_op | source)
XLA Modules:
  0.0 96.5 jit_solution(17317944227717198725)
XLA Ops:
  0.6 0.0 copy-start
  0.6 0.0 copy-start.1
  0.7 0.0 copy-start.2
  0.7 0.0 copy-start.3
  0.7 1.6 %edges.1 = (f32[2,32,128]{2,1,0:T(8,128)S(1)}, f32[2,32,128]{2,1,0:T(8,128)S(1)}, f32[2,32,128]{2,1,0:T(8,128)S(1)}, f32[2,32,128]{2,1,0:T(8,128)S(1)}, s32[32,3...) custom-call(f32[32,32,128]{2,1,0:T(8,128)} %tracer.3, bf16[32,32,128]{2,1,0:T(8,128)(2,1)} %wind_x.3, ...), custom_call_target="tpu_custom_call" | custom-call | bytes 524288 | tf_op jit(solution)/shard_map/edges/pallas_call | solution.py:16
  2.2 0.0 collective-permute-start
  2.3 1.7 %collective-permute-start.1 = (f32[2,32,128]{2,1,0:T(8,128)S(1)}, f32[2,32,128]{2,1,0:T(8,128)S(1)}, u32[]{:S(2)}, u32[]{:S(2)}) collective-permute-start(f32[2,32,128]{2,1,0:T(8,128)S(1)} %get-tuple-element.16), channel_id=1, source_target_pairs={{64,0},{128,64},{192,128},{256,192},{320,256},{384,320},{448,384},... | collective-permute-start | bytes 98312 | tf_op jit(solution)/shard_map/ppermute | solution.py:296
  4.0 3.6 %collective-permute-start.2 = (f32[2,32,128]{2,1,0:T(8,128)S(1)}, f32[2,32,128]{2,1,0:T(8,128)S(1)}, u32[]{:S(2)}, u32[]{:S(2)}) collective-permute-start(f32[2,32,128]{2,1,0:T(8,128)S(1)} %get-tuple-element.17), channel_id=1, source_target_pairs={{0,1},{1,2},{2,3},{3,4},{4,5},{5,6},{6,7},{7,8},{8,9},{9,10},{10,1... | collective-permute-start | bytes 98312 | tf_op jit(solution)/shard_map/ppermute | solution.py:298
  7.6 19.3 %collective-permute-start.3 = (f32[2,32,128]{2,1,0:T(8,128)S(1)}, f32[2,32,128]{2,1,0:T(8,128)S(1)}, u32[]{:S(2)}, u32[]{:S(2)}) collective-permute-start(f32[2,32,128]{2,1,0:T(8,128)S(1)} %get-tuple-element.18), channel_id=1, source_target_pairs={{1,0},{2,1},{3,2},{4,3},{5,4},{6,5},{7,6},{8,7},{9,8},{10,9},{11,1... | collective-permute-start | bytes 98312 | tf_op jit(solution)/shard_map/ppermute | solution.py:299
  27.0 0.0 collective-permute-done.west
  27.0 0.0 collective-permute-done.1.east
  27.0 0.0 collective-permute-done.2.south
  27.0 1.6 %collective-permute-done.3.north = f32[2,32,128]{2,1,0:T(8,128)S(1)} collective-permute-done((f32[2,32,128]{2,1,0:T(8,128)S(1)}, f32[2,32,128]{2,1,0:T(8,128)S(1)}, u32[]{:S(2)}, u32[]{:S(2)}) %collective-permute-start.3) | collective-permute-done | bytes 32800 | tf_op jit(solution)/shard_map/ppermute | solution.py:299
  28.6 0.0 copy-done
  28.6 0.0 copy-done.3
  28.6 0.0 copy-start.5
  28.6 0.0 copy-start.6
  28.6 3.2 %advect.1 = (f32[32,32,128]{2,1,0:T(8,128)S(1)}, bf16[1024,512]{1,0:T(8,128)(2,1)S(1)}, bf16[1024,1024]{1,0:T(8,128)(2,1)S(1)}) custom-call(f32[32,32,128]{2,1,0:T(8,128)S(1)} %copy-done, bf16[32,32,128]{2,1,0:T(8,128)(2,1)S(1)} %copy-done.1, bf16[32,32,128]{2,1,0:T(8,128)(2,1)S(1)} %copy-done.2, f32[32,32]{1,0:T(8,128)S(1)} %copy-done.3, ...), custom_call_target="tpu_custom_call" | custom-call | flops 268435456 | bytes 6291456 | tf_op jit(solution)/shard_map/advect/pallas_call | solution.py:16
  31.8 0.0 copy-start.4
  31.9 36.2 %all_to_all.10 = bf16[64,16,512]{2,1,0:T(8,128)(2,1)S(1)} all-to-all(bf16[64,16,512]{2,1,0:T(8,128)(2,1)S(1)} %bitcast.7), channel_id=1, replica_groups=mesh['face'=16,'blk'=64] {'blk'}, dimensions={0} | all-to-all | bytes 2097152 | tf_op jit(solution)/shard_map/all_to_all | solution.py:338
  68.0 0.0 copy-done.5
  68.0 3.2 %net.1 = (bf16[1024,256]{1,0:T(8,128)(2,1)S(1)}, f32[32,32,128]{2,1,0:T(8,128)}) custom-call(bf16[1024,512]{1,0:T(8,128)(2,1)S(1)} %bitcast.8, bf16[1,512,512]{2,1,0:T(8,128)(2,1)S(1)} %copy-done.5, bf16[1,4,512,512]{3,2,1,0:T(8,128)(2,1)S(1)} %copy-done.4, bf16[1,512,256]{2,1,0:T(8,128)(2,1)S(1)} %copy-done.6, f32[32,32,128]{2,1,0:T(8,128)S(1)} %get-tuple-element.24.advected), custom_call_target="tpu_custom_call" | custom-call | flops 2952790016 | bytes 5242880 | tf_op jit(solution)/shard_map/net/pallas_call | solution.py:16
  71.2 23.7 %all_to_all.11 = bf16[64,16,256]{2,1,0:T(8,128)(2,1)S(1)} all-to-all(bf16[64,16,256]{2,1,0:T(8,128)(2,1)S(1)} %bitcast.9), channel_id=1, replica_groups=mesh['face'=16,'blk'=64] {'blk'}, dimensions={0} | all-to-all | bytes 1048576 | tf_op jit(solution)/shard_map/all_to_all | solution.py:351
  95.0 1.5 %unpack.1 = bf16[1024,256]{1,0:T(8,128)(2,1)} custom-call(s32[32,32]{1,0:T(8,128)S(1)} %get-tuple-element.19.target, bf16[1024,1024]{1,0:T(8,128)(2,1)S(1)} %get-tuple-element.26.to_columns, bf16[1024,256]{1,0:T(8,128)(2,1)S(1)} %bitcast.6), custom_call_target="tpu_custom_call" | custom-call | flops 536870912 | bytes 1048576 | tf_op jit(solution)/shard_map/unpack/pallas_call | solution.py:16
  (5 shorter events, 0.0 us)
Async XLA Ops:
  0.6 28.0 %copy-start = (f32[32,32,128]{2,1,0:T(8,128)S(1)}, f32[32,32,128]{2,1,0:T(8,128)}, u32[]{:S(2)}) copy-start(f32[32,32,128]{2,1,0:T(8,128)} %tracer.3) | copy-start | bytes 1572868
  0.6 28.0 %copy-start.1 = (bf16[32,32,128]{2,1,0:T(8,128)(2,1)S(1)}, bf16[32,32,128]{2,1,0:T(8,128)(2,1)}, u32[]{:S(2)}) copy-start(bf16[32,32,128]{2,1,0:T(8,128)(2,1)} %wind_x.3) | copy-start | bytes 786436
  0.7 28.0 %copy-start.2 = (bf16[32,32,128]{2,1,0:T(8,128)(2,1)S(1)}, bf16[32,32,128]{2,1,0:T(8,128)(2,1)}, u32[]{:S(2)}) copy-start(bf16[32,32,128]{2,1,0:T(8,128)(2,1)} %wind_y.3) | copy-start | bytes 786436
  0.7 28.0 %copy-start.3 = (f32[32,32]{1,0:T(8,128)S(1)}, f32[32,32]{1,0:T(8,128)}, u32[]{:S(2)}) copy-start(f32[32,32]{1,0:T(8,128)} %area.1) | copy-start | bytes 12292
  2.2 24.7 %collective-permute-start = (f32[2,32,128]{2,1,0:T(8,128)S(1)}, f32[2,32,128]{2,1,0:T(8,128)S(1)}, u32[]{:S(2)}, u32[]{:S(2)}) collective-permute-start(f32[2,32,128]{2,1,0:T(8,128)S(1)} %get-tuple-element.15), channel_id=1, source_target_pairs={{0,64},{64,128},{128,192},{192,256},{256,320},{320,384},{384,448},... | collective-permute-start | bytes 98312 | tf_op jit(solution)/shard_map/ppermute | solution.py:295
  2.3 24.7 %collective-permute-start.1 = (f32[2,32,128]{2,1,0:T(8,128)S(1)}, f32[2,32,128]{2,1,0:T(8,128)S(1)}, u32[]{:S(2)}, u32[]{:S(2)}) collective-permute-start(f32[2,32,128]{2,1,0:T(8,128)S(1)} %get-tuple-element.16), channel_id=1, source_target_pairs={{64,0},{128,64},{192,128},{256,192},{320,256},{384,320},{448,384},... | collective-permute-start | bytes 98312 | tf_op jit(solution)/shard_map/ppermute | solution.py:296
  4.0 23.0 %collective-permute-start.2 = (f32[2,32,128]{2,1,0:T(8,128)S(1)}, f32[2,32,128]{2,1,0:T(8,128)S(1)}, u32[]{:S(2)}, u32[]{:S(2)}) collective-permute-start(f32[2,32,128]{2,1,0:T(8,128)S(1)} %get-tuple-element.17), channel_id=1, source_target_pairs={{0,1},{1,2},{2,3},{3,4},{4,5},{5,6},{6,7},{7,8},{8,9},{9,10},{10,1... | collective-permute-start | bytes 98312 | tf_op jit(solution)/shard_map/ppermute | solution.py:298
  7.6 21.0 %collective-permute-start.3 = (f32[2,32,128]{2,1,0:T(8,128)S(1)}, f32[2,32,128]{2,1,0:T(8,128)S(1)}, u32[]{:S(2)}, u32[]{:S(2)}) collective-permute-start(f32[2,32,128]{2,1,0:T(8,128)S(1)} %get-tuple-element.18), channel_id=1, source_target_pairs={{1,0},{2,1},{3,2},{4,3},{5,4},{6,5},{7,6},{8,7},{9,8},{10,9},{11,1... | collective-permute-start | bytes 98312 | tf_op jit(solution)/shard_map/ppermute | solution.py:299
  28.6 39.4 %copy-start.5 = (bf16[1,512,512]{2,1,0:T(8,128)(2,1)S(1)}, bf16[1,512,512]{2,1,0:T(8,128)(2,1)}, u32[]{:S(2)}) copy-start(bf16[1,512,512]{2,1,0:T(8,128)(2,1)} %w_in.1) | copy-start | bytes 1572868
  28.6 39.4 %copy-start.6 = (bf16[1,512,256]{2,1,0:T(8,128)(2,1)S(1)}, bf16[1,512,256]{2,1,0:T(8,128)(2,1)}, u32[]{:S(2)}) copy-start(bf16[1,512,256]{2,1,0:T(8,128)(2,1)} %w_out.1) | copy-start | bytes 786436
  31.8 36.2 %copy-start.4 = (bf16[1,4,512,512]{3,2,1,0:T(8,128)(2,1)S(1)}, bf16[1,4,512,512]{3,2,1,0:T(8,128)(2,1)}, u32[]{:S(2)}) copy-start(bf16[1,4,512,512]{3,2,1,0:T(8,128)(2,1)} %w_hidden.1) | copy-start | bytes 6291460
